TPU v7x, 256 devices: a whole 4x4x8 slice. The times are simulated.
256 devices in a mesh: circ: 32 (over z, y_hi, core), norm: 4 (over x), span: 2 (over y_lo).
Axes of the slice: x: 4, y: 4 (y_hi: 2, y_lo: 2; y = y_hi * 2 + y_lo), z: 8, core: 2. Of those that a mesh axis runs over, the one named last changes fastest.
Arguments:
- state: float32 [5, 512, 64, 256], P(None, 'circ', 'norm', 'span'), may hold values from -6 to 6
- viscosity: float32 [512, 64, 256], P('circ', 'norm', 'span'), may hold values from 6e-05 to 0.0006
- visc_matrix: float32 [5, 5], replicated, may hold values from -2.5 to 2.5
- circ_lower_coef: float32 [512, 64, 256], P('circ', 'norm', 'span'), may hold values from 0.985 to 0.999
- circ_upper_coef: float32 [512, 64, 256], P('circ', 'norm', 'span'), may hold values from 0.985 to 0.999
- normal_lower_coef: float32 [512, 64, 256], P('circ', 'norm', 'span'), may hold values from 0.975 to 0.998
- normal_upper_coef: float32 [512, 64, 256], P('circ', 'norm', 'span'), may hold values from 0.975 to 0.998
- circ_plus: float32 [5, 5], replicated, may hold values from -0.001 to 0.992, as said below
- circ_minus: float32 [5, 5], replicated, may hold values from -0.001 to 0.992, as said below
- normal_plus: float32 [5, 5], replicated, may hold values from -0.006 to 0.975, as said below
- normal_minus: float32 [5, 5], replicated, may hold values from -0.006 to 0.975, as said below
Outputs:
- increment: float32 [5, 512, 64, 256], P(None, 'circ', 'norm', 'span')
Inputs may be any that keep to these rules, and one draw needn't show every extreme that they name: `circ_plus`: diagonal entries between 0.985 and 0.992, off-diagonal entries of magnitude at most 0.001. `circ_minus`: diagonal entries between 0.985 and 0.992, off-diagonal entries of magnitude at most 0.001. `normal_plus`: diagonal entries between 0.95 and 0.975, off-diagonal entries of magnitude at most 0.006. `normal_minus`: diagonal entries between 0.95 and 0.975, off-diagonal entries of magnitude at most 0.006.
All inputs are finite; a program needn't handle non-finite values.
Results may differ from a plain program's by a relative error of at most 0.0003.
Values sent between devices are 32-bit elements; how exact they have to be, the bound alone decides.
A program may use at most 64 MiB of HBM per device.

v0:
```python
import jax
import jax.numpy as jnp
from jax import lax
from jax.sharding import PartitionSpec as P


def prefix_2(array, axis, combine, identity, reverse):
    count, mine = (lax.axis_size(axis), lax.axis_index(axis))
    everything = jax.tree.map(lambda part: lax.all_gather(part, axis), array)
    start = jax.tree.map(
        lambda part, zero: jnp.broadcast_to(jnp.asarray(zero, part.dtype), part.shape),
        array,
        identity,
    )

    def hop(k, before):
        at = count - 1 - k if reverse else k
        reached = at > mine if reverse else at < mine
        new = combine(before, jax.tree.map(lambda part: part[at], everything))
        return jax.tree.map(lambda a, b: jnp.where(reached, a, b), new, before)

    return lax.fori_loop(0, count, hop, start)


def spread(block, axis, source):
    block = jnp.where(lax.axis_index(axis) == source, block, jnp.zeros_like(block))
    return lax.psum(block, axis)


def padded(block, sides, width, periodic):
    for axis, dim in sides:
        count = lax.axis_size(axis)
        forward = [(i, i + 1) for i in range(count - 1)]
        if periodic:
            forward.append((count - 1, 0))
        backward = [(target, source) for source, target in forward]
        low = lax.ppermute(
            lax.slice_in_dim(block, block.shape[dim] - width, None, axis=dim), axis, forward
        )
        high = lax.ppermute(lax.slice_in_dim(block, 0, width, axis=dim), axis, backward)
        block = jnp.concatenate([low, block, high], axis=dim)
    return block


def apply_matrix(mat, vec):
    return jnp.einsum("ab,bxy->axy", mat, vec, precision=lax.Precision.HIGHEST)


def power_of(mat, count):
    result = jnp.eye(mat.shape[0], dtype=jnp.float32)
    base = mat
    while count > 0:
        if count % 2 == 1:
            result = jnp.dot(result, base, precision=lax.Precision.HIGHEST)
        base = jnp.dot(base, base, precision=lax.Precision.HIGHEST)
        count = count // 2
    return result


def solve_five(scale, jmat, vec):
    size = jmat.shape[0]
    rows = [
        [(1.0 if r == c else 0.0) - scale * jmat[r, c] for c in range(size)] for r in range(size)
    ]
    right = [vec[r] for r in range(size)]
    for k in range(size):
        for r in range(k + 1, size):
            factor = rows[r][k] / rows[k][k]
            for c in range(k + 1, size):
                rows[r][c] = rows[r][c] - factor * rows[k][c]
            right[r] = right[r] - factor * right[k]
    result = [None] * size
    for r in range(size - 1, -1, -1):
        total = right[r]
        for c in range(r + 1, size):
            total = total - rows[r][c] * result[c]
        result[r] = total / rows[r][r]
    return jnp.stack(result, 0)


def sweep(field, coef, mat, start, axis, backward):
    items = (jnp.moveaxis(field, axis, 0), jnp.moveaxis(coef, axis - 1, 0))

    def step(carry, item):
        value, scale = item
        carry = value + scale[None] * apply_matrix(mat, carry)
        return (carry, carry)

    last, values = lax.scan(step, start, items, reverse=backward)
    return (jnp.moveaxis(values, 0, axis), last)


def compose(earlier, later):
    mat_early, scale_early, shift_early = earlier
    mat_late, scale_late, shift_late = later
    joined = jnp.dot(mat_late, mat_early, precision=lax.Precision.HIGHEST)
    return (
        joined,
        scale_early * scale_late,
        scale_late[None] * apply_matrix(mat_late, shift_early) + shift_late,
    )


def apply_map(mapping, vec):
    return mapping[1][None] * apply_matrix(mapping[0], vec) + mapping[2]


def identity_of(own):
    return (
        jnp.eye(own[0].shape[0], dtype=jnp.float32),
        jnp.ones_like(own[1]),
        jnp.zeros_like(own[2]),
    )


def circ_sweep(field, coef, mat, backward):
    zero = jnp.zeros((field.shape[0], field.shape[2], field.shape[3]), jnp.float32)
    _, last = sweep(field, coef, mat, zero, 1, backward)
    own = (power_of(mat, field.shape[1]), jnp.prod(coef, axis=0), last)
    prefix = prefix_2(own, "circ", compose, identity_of(own), backward)
    total = compose(prefix, own)
    closing = solve_five(total[1], total[0], total[2])
    root = 0 if backward else lax.axis_size("circ") - 1
    closing = spread(closing, "circ", root)
    start = apply_map(prefix, closing)
    values, _ = sweep(field, coef, mat, start, 1, backward)
    return values


def normal_sweep(field, coef, mat, backward):
    zero = jnp.zeros((field.shape[0], field.shape[1], field.shape[3]), jnp.float32)
    _, last = sweep(field, coef, mat, zero, 2, backward)
    own = (power_of(mat, field.shape[2]), jnp.prod(coef, axis=1), last)
    prefix = prefix_2(own, "norm", compose, identity_of(own), backward)
    values, _ = sweep(field, coef, mat, prefix[2], 2, backward)
    return values


def per_device(
    state,
    viscosity,
    visc_matrix,
    circ_lower_coef,
    circ_upper_coef,
    normal_lower_coef,
    normal_upper_coef,
    circ_plus,
    circ_minus,
    normal_plus,
    normal_minus,
):
    wrapped = padded(state, (("circ", 1), ("span", 3)), 1, True)
    beside_all = wrapped[:, 2:, :, 1:-1] + wrapped[:, :-2, :, 1:-1]
    across = wrapped[:, 1:-1, :, 2:] + wrapped[:, 1:-1, :, :-2]
    walled = padded(state, (("norm", 2),), 1, False)
    outward = walled[:, :, 2:] + walled[:, :, :-2]
    lap = beside_all + across + outward - 6.0 * state
    rhs = viscosity[None] * apply_matrix(
        visc_matrix, lap.reshape(lap.shape[0], lap.shape[1], -1)
    ).reshape(lap.shape)
    lower_circ = circ_sweep(rhs, circ_lower_coef, circ_plus, False)
    upper_circ = circ_sweep(lower_circ, circ_upper_coef, circ_minus, True)
    lower_normal = normal_sweep(upper_circ, normal_lower_coef, normal_plus, False)
    increment = normal_sweep(lower_normal, normal_upper_coef, normal_minus, True)
    return increment


def solution(mesh):
    placed = (
        P(None, "circ", "norm", "span"),
        P("circ", "norm", "span"),
        P(),
        P("circ", "norm", "span"),
        P("circ", "norm", "span"),
        P("circ", "norm", "span"),
        P("circ", "norm", "span"),
        P(),
        P(),
        P(),
        P(),
    )
    return jax.shard_map(
        per_device,
        mesh=mesh,
        in_specs=placed,
        out_specs=P(None, "circ", "norm", "span"),
        check_vma=False,
    )
```

profile of v0, /device:TPU:1, one launch (start us, length us, event | category | flops | bytes accessed | tf_op | source)
XLA Modules:
  0.0 720.0 jit_solution(3760572138266239184)
XLA Ops:
  7.4 4.3 collective-permute-start.1
  12.8 1.3 collective-permute-start.4
  14.1 4.0 collective-permute-start.5
  24.7 1.4 fusion.80
  26.2 1.2 reshape.11
  27.4 1.4 convolution_bitcast_fusion
  30.6 4.0 while.180
  36.3 48.1 %all-gather.15 = f32[32,5,5]{2,1,0:T(8,128)S(1)} all-gather(f32[1,5,5]{2,1,0:T(8,128)S(1)} %bitcast.471), channel_id=8, replica_groups=mesh['circ'=32,'norm'=4,'span'=2] {'circ'}, dimensions={0}, use_global_device_ids=true | all-gather | bytes 3300 | tf_op jit(solution)/shard_map/all_gather | solution.py:9
  84.4 37.5 %all-gather.7 = f32[512,128]{1,0:T(8,128)S(1)} all-gather(f32[16,128]{1,0:T(8,128)S(1)} %reduce_prod.39), channel_id=9, replica_groups=mesh['circ'=32,'norm'=4,'span'=2] {'circ'}, dimensions={0}, use_global_device_ids=true | all-gather | bytes 270336 | tf_op jit(solution)/shard_map/all_gather | solution.py:9
  122.3 37.2 %while.181 = (s32[]{:T(128)}, f32[5,5]{1,0:T(8,128)S(1)}, f32[16,128]{1,0:T(8,128)S(1)}, f32[5,16,128]{2,0,1:T(8,128)S(1)}, s32[]{:T(128)}, /*index=5*/f32[32,5,...) while((s32[]{:T(128)}, f32[5,5]{1,0:T(8,128)S(1)}, ...), condition=%wide.region_7.8_spmd.clone, body=%wide.region_6.7_spmd.clone.sunk | while | flops 673273 | bytes 436150 | solution.py:22
  161.2 15.5 %constant_dynamic-update-slice_fusion.7 = (f32[5,16,128]{2,1,0:T(8,128)S(1)}, f32[16,128]{1,0:T(8,128)S(1)}, f32[16,128]{1,0:T(8,128)S(1)}, f32[16,128]{1,0:T(8,128)S(1)}, f32[16,128]{1,0:T(8,128)S(1)}) fusion(f32[16,128]{1,0:T(8,128)S(1)} %bitcast.468, f32[]{:T(128)} %bitcast.52, f32[]{:T(128)} %bitcast.44, f32[]{:T(128)} %bitcast.38, f32[]{:T(128)} %bitcast.36, ...), kind=kLoop, calls=%fused_computation.150 | loop fusion | flops 339967 | bytes 98404
  176.8 6.2 constant_dynamic-update-slice_fusion.6
  183.1 125.8 %psum.14 = f32[5,16,128]{2,1,0:T(8,128)S(1)} all-reduce(f32[5,16,128]{2,1,0:T(8,128)S(1)} %broadcast_select_fusion.1), channel_id=1, replica_groups=mesh['circ'=32,'norm'=4,'span'=2] {'circ'}, use_global_device_ids=true, to_apply=%region_8.9 | all-reduce | flops 10240 | bytes 81920 | tf_op jit(solution)/shard_map/psum | solution.py:27
  309.2 4.0 while.176
  313.2 4.0 while.182
  318.2 9.4 %all-gather.13 = f32[4,5,5]{2,1,0:T(8,128)S(1)} all-gather(f32[1,5,5]{2,1,0:T(8,128)S(1)} %convolution_bitcast_fusion.1), channel_id=5, replica_groups=mesh['circ'=32,'norm'=4,'span'=2] {'norm'}, dimensions={0}, use_global_device_ids=true | all-gather | bytes 500 | tf_op jit(solution)/shard_map/all_gather | solution.py:9
  328.2 9.1 %all-gather.12 = f32[4,5,5]{2,1,0:T(8,128)S(1)} all-gather(f32[1,5,5]{2,1,0:T(8,128)S(1)} %convolution_bitcast_fusion.2), channel_id=3, replica_groups=mesh['circ'=32,'norm'=4,'span'=2] {'norm'}, dimensions={0}, use_global_device_ids=true | all-gather | bytes 500 | tf_op jit(solution)/shard_map/all_gather | solution.py:9
  337.9 48.4 %all-gather.14 = f32[32,5,5]{2,1,0:T(8,128)S(1)} all-gather(f32[1,5,5]{2,1,0:T(8,128)S(1)} %bitcast.470), channel_id=6, replica_groups=mesh['circ'=32,'norm'=4,'span'=2] {'circ'}, dimensions={0}, use_global_device_ids=true | all-gather | bytes 3300 | tf_op jit(solution)/shard_map/all_gather | solution.py:9
  386.3 9.4 %all-gather.2 = f32[64,128]{1,0:T(8,128)S(1)} all-gather(f32[16,128]{1,0:T(8,128)S(1)} %reduce_prod.37), channel_id=4, replica_groups=mesh['circ'=32,'norm'=4,'span'=2] {'norm'}, dimensions={0}, use_global_device_ids=true | all-gather | bytes 40960 | tf_op jit(solution)/shard_map/all_gather | solution.py:9
  395.8 9.0 %all-gather = f32[64,128]{1,0:T(8,128)S(1)} all-gather(f32[16,128]{1,0:T(8,128)S(1)} %reduce_prod.36), channel_id=2, replica_groups=mesh['circ'=32,'norm'=4,'span'=2] {'norm'}, dimensions={0}, use_global_device_ids=true | all-gather | bytes 40960 | tf_op jit(solution)/shard_map/all_gather | solution.py:9
  404.8 46.1 %all-gather.5 = f32[512,128]{1,0:T(8,128)S(1)} all-gather(f32[16,128]{1,0:T(8,128)S(1)} %reduce_prod.38), channel_id=7, replica_groups=mesh['circ'=32,'norm'=4,'span'=2] {'circ'}, dimensions={0}, use_global_device_ids=true | all-gather | bytes 270336 | tf_op jit(solution)/shard_map/all_gather | solution.py:9
  450.9 37.2 %while.183 = (s32[]{:T(128)}, f32[5,5]{1,0:T(8,128)S(1)}, f32[16,128]{1,0:T(8,128)S(1)}, f32[5,16,128]{2,0,1:T(8,128)S(1)}, s32[]{:T(128)}, /*index=5*/f32[32,5,...) while((s32[]{:T(128)}, f32[5,5]{1,0:T(8,128)S(1)}, ...), condition=%wide.region_14.15_spmd.clone, body=%wide.region_13.14_spmd.clone.sunk | while | flops 673277 | bytes 436720 | solution.py:22
  489.8 15.5 %constant_dynamic-update-slice_fusion.12 = (f32[5,16,128]{2,1,0:T(8,128)S(1)}, f32[16,128]{1,0:T(8,128)S(1)}, f32[16,128]{1,0:T(8,128)S(1)}, f32[16,128]{1,0:T(8...) fusion(f32[5,16,128]{2,1,0:T(8,128)S(1)} %fusion.87, f32[]{:T(128)} %bitcast.90, f32[]{:T(128)} %bitcast.82, ...), kind=kLoop, calls=%fused_computation.155 | loop fusion | flops 339967 | bytes 106596
  505.4 6.2 constant_dynamic-update-slice_fusion.11
  511.7 123.0 %psum.15 = f32[5,16,128]{2,1,0:T(8,128)S(1)} all-reduce(f32[5,16,128]{2,1,0:T(8,128)S(1)} %broadcast_select_fusion), channel_id=1, replica_groups=mesh['circ'=32,'norm'=4,'span'=2] {'circ'}, use_global_device_ids=true, to_apply=%region_15.16 | all-reduce | flops 10240 | bytes 81920 | tf_op jit(solution)/shard_map/psum | solution.py:27
  635.0 4.0 while.177
  639.0 4.0 while.184
  643.0 9.2 %all-gather.10 = f32[20,16,128]{2,1,0:T(8,128)S(1)} all-gather(f32[5,16,128]{2,1,0:T(8,128)S(1)} %copy.180), channel_id=12, replica_groups=mesh['circ'=32,'norm'=4,'span'=2] {'norm'}, dimensions={0}, use_global_device_ids=true | all-gather | bytes 204800 | tf_op jit(solution)/shard_map/all_gather | solution.py:9
  653.4 4.0 while.178
  657.4 4.0 while.186
  661.5 9.2 %all-gather.11 = f32[20,16,128]{2,1,0:T(8,128)S(1)} all-gather(f32[5,16,128]{2,1,0:T(8,128)S(1)} %copy.183), channel_id=13, replica_groups=mesh['circ'=32,'norm'=4,'span'=2] {'norm'}, dimensions={0}, use_global_device_ids=true | all-gather | bytes 204800 | tf_op jit(solution)/shard_map/all_gather | solution.py:9
  671.8 40.5 %while.179 = (s32[]{:T(128)}, f32[5,16,128]{2,0,1:T(8,128)S(1)}, f32[16,5,16,128]{3,0,2,1:T(8,128)S(1)}, f32[16,5,16,128]{3,1,2,0:T(8,128)S(1)}, f32[16,16,128]{...) while((s32[]{:T(128)}, f32[5,16,128]{2,0,1:T(8,128)S(1)}, ...), condition=%wide.region_29.30_spmd, body=%wide.region_28.29_spmd.sunk | while | flops 634883 | bytes 393433 | solution.py:89
  672.1 2.2 dynamic_update_slice.35
  674.6 2.2 dynamic_update_slice.35
  677.2 2.2 dynamic_update_slice.35
  679.7 2.2 dynamic_update_slice.35
  682.2 2.2 dynamic_update_slice.35
  684.8 2.2 dynamic_update_slice.35
  687.3 2.2 dynamic_update_slice.35
  689.8 2.2 dynamic_update_slice.35
  692.4 2.2 dynamic_update_slice.35
  694.9 2.2 dynamic_update_slice.35
  697.4 2.2 dynamic_update_slice.35
  700.0 2.2 dynamic_update_slice.35
  702.5 2.2 dynamic_update_slice.35
  705.0 2.2 dynamic_update_slice.35
  707.6 2.2 dynamic_update_slice.35
  710.1 2.2 dynamic_update_slice.35
  (936 shorter events, 123.6 us)
Async XLA Ops:
  6.5 20.8 %copy-start = (f32[5,5]{1,0:T(8,128)S(1)}, f32[5,5]{1,0:T(8,128)}, u32[]{:S(2)}) copy-start(f32[5,5]{1,0:T(8,128)} %param.37) | copy-start | bytes 304
  6.5 115.7 %all-gather.19.cloned.1.call-start = ((), (), s32[]{:S(2)}) async-start(), calls=%async_computation | async-start | bytes 1351680 | tf_op jit(solution)/shard_map/all_gather | solution.py:9
  7.4 10.7 %collective-permute-start.1 = (f32[5,1,16,128]{3,2,1,0:T(8,128)S(1)}, f32[5,1,16,128]{3,2,1,0:T(8,128)S(1)}, u32[]{:S(2)}, u32[]{:S(2)}) collective-permute-start(f32[5,1,16,128]{3,2,1,0:T(8,128)S(1)} %get-tuple-element.1724), channel_id=1, source_target_pairs={{0,8},{8,16},{16,24},{24,32},{32,40},{40,48},{48,56},{56,64},{64,7... | collective-permute-start | bytes 122888 | tf_op jit(solution)/shard_map/ppermute | solution.py:37
  11.7 7.6 %collective-permute-start = (f32[5,1,16,128]{3,2,1,0:T(8,128)S(1)}, f32[5,1,16,128]{3,2,1,0:T(8,128)S(1)}, u32[]{:S(2)}, u32[]{:S(2)}) collective-permute-start(f32[5,1,16,128]{3,2,1,0:T(8,128)S(1)} %get-tuple-element.1723), channel_id=1, source_target_pairs={{8,0},{16,8},{24,16},{32,24},{40,32},{48,40},{56,48},{64,56},{72,6... | collective-permute-start | bytes 122888 | tf_op jit(solution)/shard_map/ppermute | solution.py:40
  12.8 11.9 %collective-permute-start.4 = (f32[5,16,1,128]{3,1,2,0:T(8,128)S(1)}, f32[5,16,1,128]{3,1,2,0:T(8,128)S(1)}, u32[]{:S(2)}, u32[]{:S(2)}) collective-permute-start(f32[5,16,1,128]{3,1,2,0:T(8,128)S(1)} %bitcast.475), channel_id=1, source_target_pairs={{2,0},{4,2},{6,4},{3,1},{5,3},{7,5},{10,8},{12,10},{14,12},{11,9},... | collective-permute-start | bytes 122888 | tf_op jit(solution)/shard_map/ppermute | solution.py:40
  14.1 10.6 %collective-permute-start.5 = (f32[5,16,1,128]{3,1,2,0:T(8,128)S(1)}, f32[5,16,1,128]{3,1,2,0:T(8,128)S(1)}, u32[]{:S(2)}, u32[]{:S(2)}) collective-permute-start(f32[5,16,1,128]{3,1,2,0:T(8,128)S(1)} %bitcast.474), channel_id=1, source_target_pairs={{0,2},{2,4},{4,6},{1,3},{3,5},{5,7},{8,10},{10,12},{12,14},{9,11},... | collective-permute-start | bytes 122888 | tf_op jit(solution)/shard_map/ppermute | solution.py:37
  20.1 4.6 copy-start.1
  20.1 3.2 collective-permute-start.2
  21.2 2.9 collective-permute-start.3
  28.7 0.9 copy-start.11
  29.6 0.7 copy-start.3
  29.6 0.9 copy-start.9
  30.6 4.8 copy-start.7
  30.6 4.9 copy-start.8
  30.6 5.1 copy-start.10
  34.6 87.3 %copy-start.5 = (f32[5,5]{1,0:T(8,128)S(1)}, f32[5,5]{1,0:T(8,128)}, u32[]{:S(2)}) copy-start(f32[5,5]{1,0:T(8,128)} %param.44) | copy-start | bytes 304
  35.2 415.7 %all-gather.21.cloned.1.call-start = ((), (), s32[]{:S(2)}) async-start(), calls=%async_computation.1 | async-start | bytes 1351680 | tf_op jit(solution)/shard_map/all_gather | solution.py:9
  309.2 4.0 copy-start.4
  313.2 14.4 %copy-start.6 = (f32[5,5]{1,0:T(8,128)S(1)}, f32[5,5]{1,0:T(8,128)}, u32[]{:S(2)}) copy-start(f32[5,5]{1,0:T(8,128)} %param.45) | copy-start | bytes 304
  712.4 0.8 copy-start.2
Sparse Core Ops, SparseCore 0:
  35.3 84.1 all-gather.18
  318.0 79.3 all-gather.20
where the time goes:
time: 734 us; the launch traced here: 720 us
  blocking collectives  484 us (66%)
  local copies, waits for them, and re-layouts  103 us (14%)
  matrix products  52.9 us (7%)
  other arithmetic  45.6 us (6%)
  between operations  14 us (2%)
  starting transfers between devices  11.2 us (2%)
  loops' own time  7.64 us (1%)
    psum x2, blocking collectives, spread(): return lax.psum(block, axis)  249 us
    all_gather x10, blocking collectives, prefix_2(): everything = jax.tree.map(lambda part: lax.all_gather(part, axis), array)  235 us
    dynamic_slice x72, local copies, waits for them, and re-layouts, hop(): new = combine(before, jax.tree.map(lambda part: part[at], everything))  50.5 us
    unnamed x14, other arithmetic  43.6 us
    dot_general x205, matrix products, apply_matrix(): return jnp.einsum('ab,bxy->axy', mat, vec, precision=lax.Precision.HIGHEST)  41.4 us
    dynamic_update_slice x32, local copies, waits for them, and re-layouts, sweep(): last, values = lax.scan(step, start, items, reverse=backward)  36.3 us
  transfers between devices with their start and end apart: 8, of which 2 were waited for; matrix products, arithmetic and copies ran while one was open for 1% of the time, Pallas kernels for 0%

commit v1 on v0

v1 whole, which is shorter than its diff:
```python
import jax
import jax.numpy as jnp
from jax import lax
from jax.experimental import pallas as pl
from jax.experimental.pallas import tpu as pltpu
from jax.sharding import PartitionSpec as P

MESH = pl.DeviceIdType.MESH
NV = 5
CIRC, NORM = 32, 4
STEPS = 16
LANES = 128
OWNERS = 16
STEP_UNROLL = 2


def place(seg):
    return lax.rem(seg, 4) * 8 + seg // 4


def shifted(groups, d, reverse):
    def turn(x, k):
        return pltpu.roll(x, 8 - k if reverse else k, axis=0)

    if d >= 4:
        return [turn(x, d // 4) for x in groups]
    if reverse:
        return [groups[v + d] if v + d < 4 else turn(groups[v + d - 4], 1) for v in range(4)]
    return [groups[v - d] if v >= d else turn(groups[v - d + 4], 1) for v in range(4)]


def apply(mat, vec):
    out = []
    for r in range(NV):
        total = mat[r][0] * vec[0]
        for c in range(1, NV):
            total = total + mat[r][c] * vec[c]
        out.append(total)
    return out


def matmul(a, b):
    out = []
    for r in range(NV):
        for c in range(NV):
            total = a[NV * r] * b[c]
            for k in range(1, NV):
                total = total + a[NV * r + k] * b[NV * k + c]
            out.append(total)
    return out


def inverse(scale, mat):
    rows = [
        [(1.0 if r == c else 0.0) - scale * mat[r][c] for c in range(NV)] for r in range(NV)
    ]
    inv = [[None] * NV for _ in range(NV)]
    for k in range(NV):
        pivot = 1.0 / rows[k][k]
        for c in range(NV):
            rows[k][c] = pivot if c == k else rows[k][c] * pivot
        for r in range(NV):
            if r == k:
                continue
            factor = rows[r][k]
            for c in range(NV):
                if c == k:
                    rows[r][c] = -factor * pivot
                else:
                    rows[r][c] = rows[r][c] - factor * rows[k][c]
    return rows


def scalars(ref):
    return [[ref[r, c] for c in range(NV)] for r in range(NV)]


def steps(body, start, reverse=False):
    def several(t, carry):
        for u in range(STEP_UNROLL):
            i = t * STEP_UNROLL + u
            carry = body(STEPS - 1 - i if reverse else i, carry)
        return carry

    return lax.fori_loop(0, STEPS // STEP_UNROLL, several, start)


def each(count, body):
    def one(k, carry):
        body(k)
        return carry

    lax.fori_loop(0, count, one, 0)


def kernel(
    state, visc_in, cl_in, cu_in, nl_in, nu_in, vm_in, cp_in, cm_in, np_in, nm_in,
    out,
    field, visc, cl, cu, nl, nu, rhs, low, turned, low_t,
    edge, edge_in, w_own, b_own, w_all, b_all, back, back_in,
    power, k_circ, k_norm, level, r_circ, a_low, a_up, g_low, g_up, m_norm, w_norm, rn, bn,
    load_sem, tl_sem, tu_sem, self_sem,
    halo_send, halo_recv, w_send, w_recv, b_send, b_recv, p_send, p_recv,
    rn_send, rn_recv, bl_send, bl_recv, bu_send, bu_recv,
):
    c, n, s = lax.axis_index("circ"), lax.axis_index("norm"), lax.axis_index("span")
    owner = lax.rem(c, 2) == 0
    row = c // 2
    zero = jnp.zeros((STEPS, LANES), jnp.float32)
    one = jnp.ones((STEPS, LANES), jnp.float32)

    def remote(src, dst, send, recv, to):
        return pltpu.make_async_remote_copy(
            src_ref=src, dst_ref=dst, send_sem=send, recv_sem=recv, device_id=to, device_id_type=MESH
        )

    barrier = pltpu.get_barrier_semaphore()

    def greet(d):
        to = lax.rem(c + d + 1, CIRC)

        @pl.when(jnp.logical_or(owner, lax.rem(to, 2) == 0))
        def _():
            pl.semaphore_signal(barrier, inc=1, device_id=(to, n, s), device_id_type=MESH)

    each(CIRC - 1, greet)
    for d in range(1, NORM):
        pl.semaphore_signal(
            barrier, inc=1, device_id=(c, lax.rem(n + d, NORM), s), device_id_type=MESH
        )
    pl.semaphore_signal(barrier, inc=1, device_id=(c, n, 1 - s), device_id_type=MESH)

    inside = pltpu.make_async_copy(
        state, field.at[:, pl.ds(1, STEPS), pl.ds(0, STEPS)], load_sem.at[0]
    )
    loads = [
        pltpu.make_async_copy(src, dst, load_sem.at[1 + k])
        for k, (src, dst) in enumerate(((cl_in, cl), (cu_in, cu), (visc_in, visc)))
    ]
    inside.start()
    for copy in loads:
        copy.start()

    def turn(src, dst, sem, j):
        return pltpu.make_async_copy(src.at[:, j], dst.at[j], sem.at[j])

    def fetch(j):
        turn(nl_in, nl, tl_sem, j).start()
        turn(nu_in, nu, tu_sem, j).start()

    each(STEPS, fetch)

    lane8 = lax.broadcasted_iota(jnp.int32, (8, LANES), 1)
    sub8 = lax.broadcasted_iota(jnp.int32, (8, LANES), 0)
    group = lane8 // 32
    base = []
    for r in range(NV):
        for k in range(NV):
            base.append(
                jnp.where(
                    group == 0,
                    cp_in[r, k],
                    jnp.where(group == 1, cm_in[r, k], jnp.where(group == 2, np_in[r, k], nm_in[r, k])),
                )
            )

    def square(t, mat):
        for e in range(NV * NV):
            power[t, e] = mat[e]
        return tuple(matmul(mat, mat))

    last = lax.fori_loop(0, 9, square, tuple(base))
    for e in range(NV * NV):
        power[9, e] = last[e]

    def kept(t):
        return [power[t, e] for e in range(NV * NV)]

    run = [
        jnp.where(sub8 % 2 == 1, base[e], 1.0 if e % (NV + 1) == 0 else 0.0) for e in range(NV * NV)
    ]
    for bit in (1, 2):
        more = matmul(run, kept(bit))
        run = [jnp.where((sub8 // (1 << bit)) % 2 == 1, more[e], run[e]) for e in range(NV * NV)]
    for half in range(2):
        if half == 1:
            run = matmul(run, kept(3))
        ahead = matmul(run, kept(0))
        both = matmul(run, [pltpu.roll(x, 32, axis=1) for x in ahead])
        for e in range(NV * NV):
            k_circ[e, pl.ds(8 * half, 8)] = jnp.broadcast_to(both[e][:, 32:33], (8, LANES))
            k_norm[e, pl.ds(8 * half, 8)] = jnp.broadcast_to(both[e][:, 96:97], (8, LANES))

    def spread(t, carry):
        for e in range(NV * NV):
            mat = power[4 + t, e]
            level[t, e] = jnp.broadcast_to(mat[:, 0:1], (8, LANES))
            level[6 + t, e] = jnp.broadcast_to(mat[:, 32:33], (8, LANES))
        return carry

    lax.fori_loop(0, 6, spread, 0)
    for e in range(NV * NV):
        m_norm[0, e] = jnp.broadcast_to(power[4, e][:, 64:65], (8, LANES))
        m_norm[1, e] = jnp.broadcast_to(power[4, e][:, 96:97], (8, LANES))

    def responses(weight, count, table, store):
        for v in range(count):
            w = [weight(i, v) for i in range(STEPS)]
            for e in range(NV * NV):
                total = w[0] * table[e, pl.ds(0, 1)]
                for i in range(1, STEPS):
                    total = total + w[i] * table[e, pl.ds(i, 1)]
                store(e, v, total)

    for copy in loads:
        copy.wait()

    def circ_scales(i, carry):
        p, q = carry
        p = p * cl[i]
        w_own[2 + i] = q * p
        return p, q * cu[i]

    p, q = steps(circ_scales, (one, one))
    w_own[0] = p
    w_own[1] = q

    inside.wait()
    lane = lax.broadcasted_iota(jnp.int32, (STEPS, LANES), 1)

    def slot(a, i):
        return (0, a * STEPS + i) if a < 4 else (1, i)

    def pack(i, packs):
        packs = list(packs)
        for a in range(NV):
            g, k = slot(a, i)
            mine = lax.rem(lane - 2 * k + 1 + LANES, LANES) <= 1
            moved = pltpu.roll(field[a, i + 1, pl.ds(0, STEPS)], 2 * k, axis=1)
            packs[g] = jnp.where(mine, moved, packs[g])
        return tuple(packs)

    packs = steps(pack, (zero, zero))
    for g in range(2):
        edge[g] = jnp.where(lane % 2 == 1, pltpu.roll(packs[g], 2, axis=1), packs[g])

    pl.semaphore_wait(barrier, jnp.where(owner, CIRC - 1, OWNERS) + NORM)

    to_next = remote(
        field.at[:, STEPS, pl.ds(0, STEPS)], field.at[:, 0, pl.ds(0, STEPS)],
        halo_send.at[0], halo_recv.at[0], (lax.rem(c + 1, CIRC), n, s),
    )
    to_prev = remote(
        field.at[:, 1, pl.ds(0, STEPS)], field.at[:, STEPS + 1, pl.ds(0, STEPS)],
        halo_send.at[1], halo_recv.at[1], (lax.rem(c + CIRC - 1, CIRC), n, s),
    )
    to_side = remote(edge, edge_in, halo_send.at[2], halo_recv.at[2], (c, n, 1 - s))
    to_up = remote(
        field.at[:, pl.ds(1, STEPS), STEPS - 1], field.at[:, pl.ds(1, STEPS), 23],
        halo_send.at[3], halo_recv.at[3], (c, n + 1, s),
    )
    to_down = remote(
        field.at[:, pl.ds(1, STEPS), 0], field.at[:, pl.ds(1, STEPS), STEPS],
        halo_send.at[4], halo_recv.at[4], (c, n - 1, s),
    )
    has_up, has_down = n < NORM - 1, n > 0
    to_next.start()
    to_prev.start()
    to_side.start()
    pl.when(has_up)(to_up.start)
    pl.when(has_down)(to_down.start)

    def nothing_at(at):
        def fill(i, carry):
            for a in range(NV):
                field[a, i + 1, pl.ds(at, 1)] = jnp.zeros((1, LANES), jnp.float32)
            return carry

        steps(fill, 0)

    pl.when(jnp.logical_not(has_up))(lambda: nothing_at(STEPS))
    pl.when(jnp.logical_not(has_down))(lambda: nothing_at(23))

    def to_owner(src, dst, send, recv, j):
        return remote(
            src.at[:, j], dst.at[:, place(c)], send.at[j], recv.at[c], (2 * j, n, s)
        )

    def from_segment(src, dst, send, recv, k):
        return remote(src.at[:, 0], dst.at[:, place(k)], send.at[0], recv.at[k], (c, n, s))

    def hand_in(src, dst, send, recv, k):
        def one_row(j):
            @pl.when(2 * j != c)
            def _():
                to_owner(src, dst, send, recv, j).start()

        each(OWNERS, one_row)

        @pl.when(owner)
        def _():
            pltpu.make_async_copy(src.at[:, row], dst.at[:, place(c)], self_sem.at[k]).start()

    def collected(src, dst, send, recv, k):
        def one_segment(seg):
            @pl.when(seg != c)
            def _():
                from_segment(src, dst, send, recv, seg).wait_recv()

        each(CIRC, one_segment)
        pltpu.make_async_copy(src.at[:, row], dst.at[:, place(c)], self_sem.at[k]).wait()

    hand_in(w_own, w_all, w_send, w_recv, 0)

    def fetched(j):
        turn(nl_in, nl, tl_sem, j).wait()
        turn(nu_in, nu, tu_sem, j).wait()

    each(STEPS, fetched)

    def norm_scales(j, carry):
        p, q = carry
        p = p * nl[j]
        w_norm[j] = q * p
        return p, q * nu[j]

    p, q = steps(norm_scales, (one, one))
    rn[n, 0] = p
    rn[n, 1] = q

    def keep_norm(e, v, total):
        rn[n, 2 + e, pl.ds(8 * v, 8)] = total

    responses(lambda j, v: w_norm[j, pl.ds(8 * v, 8)], 2, k_norm, keep_norm)

    def over_norm(d, buf, send, recv):
        to = lax.rem(n + d, NORM)
        return remote(buf.at[n], buf.at[n], send.at[d], recv.at[n], (c, to, s))

    def from_norm(d, buf, send, recv):
        k = lax.rem(n + d, NORM)
        return remote(buf.at[k], buf.at[k], send.at[d], recv.at[k], (c, k, s))

    for d in range(1, NORM):
        over_norm(d, rn, rn_send, rn_recv).start()

    to_next.wait_recv()
    to_prev.wait_recv()
    to_side.wait_recv()
    pl.when(has_up)(to_down.wait_recv)
    pl.when(has_down)(to_up.wait_recv)

    vm, cp, cm = scalars(vm_in), scalars(cp_in), scalars(cm_in)

    def sweep_step(value, scale, mat, carry):
        moved = apply(mat, carry)
        return tuple(value[a] + scale * moved[a] for a in range(NV))

    def first_low(i, carry):
        lap = []
        for a in range(NV):
            tall = field[a, i + 1]
            mid = tall[:STEPS]
            wall = pltpu.roll(tall, 1, axis=0)[:STEPS] + pltpu.roll(tall, 23, axis=0)[:STEPS]
            g, k = slot(a, i)
            beyond = pltpu.roll(edge_in[g], LANES - 1 - 2 * k, axis=1)
            left = jnp.where(lane == 0, beyond, pltpu.roll(mid, 1, axis=1))
            right = jnp.where(lane == LANES - 1, beyond, pltpu.roll(mid, LANES - 1, axis=1))
            around = field[a, i, pl.ds(0, STEPS)] + field[a, i + 2, pl.ds(0, STEPS)]
            lap.append(around + (left + right) + wall - 6.0 * mid)
        mixed = apply(vm, lap)
        value = [visc[i] * x for x in mixed]
        for a in range(NV):
            rhs[a, i] = value[a]
        carry = sweep_step(value, cl[i], cp, carry)
        for a in range(NV):
            low[a, i] = carry[a]
        return carry

    zeros = (zero,) * NV
    end = steps(first_low, zeros)
    for a in range(NV):
        b_own[a] = end[a]

    def first_up(i, carry):
        return sweep_step([low[a, i] for a in range(NV)], cu[i], cm, carry)

    end = steps(first_up, zeros, reverse=True)
    for a in range(NV):
        b_own[NV + a] = end[a]
    hand_in(b_own, b_all, b_send, b_recv, 1)

    def quad(ref, *at):
        return [ref[(*at, pl.ds(8 * v, 8))] for v in range(4)]

    def table(ref, *at):
        return [[ref[(*at, NV * r + k)] for k in range(NV)] for r in range(NV)]

    def to_segment(k):
        return remote(
            back.at[:, place(k)], back_in.at[:, row], p_send.at[k], p_recv.at[row], (k, n, s)
        )

    def from_owner(j):
        return remote(back.at[:, 0], back_in.at[:, j], p_send.at[0], p_recv.at[j], (2 * j, n, s))

    @pl.when(owner)
    def _():
        collected(w_own, w_all, w_send, w_recv, 0)

        def keep_circ(e, v, total):
            r_circ[e, pl.ds(8 * v, 8)] = total

        responses(lambda i, v: w_all[2 + i, pl.ds(8 * v, 8)], 4, k_circ, keep_circ)
        for side, (store, inv) in enumerate(((a_low, g_low), (a_up, g_up))):
            scale = quad(w_all, side)
            for t in range(5):
                for v in range(4):
                    store[t, pl.ds(8 * v, 8)] = scale[v]
                beside = shifted(scale, 1 << t, side == 1)
                scale = [scale[v] * beside[v] for v in range(4)]
            solved = inverse(scale[0], table(level, 6 * side + 5))
            for r in range(NV):
                for k in range(NV):
                    inv[NV * r + k] = solved[r][k]

        collected(b_own, b_all, b_send, b_recv, 1)

        def closed(shift, side, store, inv):
            for t in range(5):
                beside = [shifted(x, 1 << t, side == 1) for x in shift]
                scale = quad(store, t)
                mat = table(level, 6 * side + t)
                moved = [apply(mat, [beside[a][v] for a in range(NV)]) for v in range(4)]
                shift = [
                    [shift[a][v] + scale[v] * moved[v][a] for v in range(4)] for a in range(NV)
                ]
            mat = table(inv)
            solved = [apply(mat, [shift[a][v] for a in range(NV)]) for v in range(4)]
            return [shifted([solved[v][a] for v in range(4)], 1, side == 1) for a in range(NV)]

        enter = closed([quad(b_all, a) for a in range(NV)], 0, a_low, g_low)
        for a in range(NV):
            for v in range(4):
                back[a, pl.ds(8 * v, 8)] = enter[a][v]
        shift = [quad(b_all, NV + a) for a in range(NV)]
        for r in range(NV):
            for k in range(NV):
                response = quad(r_circ, NV * r + k)
                shift[r] = [shift[r][v] + response[v] * enter[k][v] for v in range(4)]
        enter = closed(shift, 1, a_up, g_up)
        for a in range(NV):
            for v in range(4):
                back[NV + a, pl.ds(8 * v, 8)] = enter[a][v]

        def give(k):
            @pl.when(k != c)
            def _():
                to_segment(k).start()

        each(CIRC, give)
        own = pltpu.make_async_copy(back.at[:, place(c)], back_in.at[:, row], self_sem.at[2])
        own.start()
        own.wait()

    def given(j):
        @pl.when(2 * j != c)
        def _():
            from_owner(j).wait_recv()

    each(OWNERS, given)

    def second_low(i, carry):
        carry = sweep_step([rhs[a, i] for a in range(NV)], cl[i], cp, carry)
        for a in range(NV):
            low[a, i] = carry[a]
        return carry

    steps(second_low, tuple(back_in[a] for a in range(NV)))

    def second_up(i, carry):
        carry = sweep_step([low[a, i] for a in range(NV)], cu[i], cm, carry)
        for a in range(NV):
            turned[a, pl.ds(i, STEPS, stride=STEPS)] = carry[a]
        return carry

    steps(second_up, tuple(back_in[NV + a] for a in range(NV)), reverse=True)

    nplus, nminus = scalars(np_in), scalars(nm_in)

    def across(j):
        return [turned[a, pl.ds(pl.multiple_of(j * STEPS, STEPS), STEPS)] for a in range(NV)]

    def norm_low(j, carry):
        carry = sweep_step(across(j), nl[j], nplus, carry)
        for a in range(NV):
            low_t[a, j] = carry[a]
        return carry

    def norm_up(j, carry):
        return sweep_step([low_t[a, j] for a in range(NV)], nu[j], nminus, carry)

    bl, bu = bn.at[0], bn.at[1]
    end = steps(norm_low, zeros)
    for a in range(NV):
        bn[0, n, a] = end[a]
    for d in range(1, NORM):
        @pl.when(n < NORM - 1)
        def _():
            over_norm(d, bl, bl_send, bl_recv).start()

    end = steps(norm_up, zeros, reverse=True)
    for a in range(NV):
        bn[1, n, a] = end[a]
    for d in range(1, NORM):
        @pl.when(lax.rem(n + d, NORM) < n)
        def _():
            over_norm(d, bu, bu_send, bu_recv).start()

    for d in range(1, NORM):
        k = lax.rem(n + d, NORM)
        from_norm(d, rn, rn_send, rn_recv).wait_recv()
        pl.when(k < NORM - 1)(from_norm(d, bl, bl_send, bl_recv).wait_recv)
        pl.when(k > n)(from_norm(d, bu, bu_send, bu_recv).wait_recv)

    def entering(v):
        half = pl.ds(8 * v, 8)
        plus, minus = table(m_norm, 0), table(m_norm, 1)
        x = {1: [bn[0, 0, a, half] for a in range(NV)]}
        for k in (1, 2):
            moved = apply(plus, x[k])
            x[k + 1] = [bn[0, k, a, half] + rn[k, 0, half] * moved[a] for a in range(NV)]
        y = {}
        for k in (3, 2, 1):
            value = [bn[1, k, a, half] for a in range(NV)]
            for r in range(NV):
                for a in range(NV):
                    value[r] = value[r] + rn[k, 2 + NV * r + a, half] * x[k][a]
            if k < 3:
                moved = apply(minus, y[k])
                value = [value[a] + rn[k, 1, half] * moved[a] for a in range(NV)]
            y[k - 1] = value
        none = jnp.zeros((8, LANES), jnp.float32)
        low_in, up_in = [none] * NV, [none] * NV
        for k in (1, 2, 3):
            low_in = [jnp.where(n == k, x[k][a], low_in[a]) for a in range(NV)]
            up_in = [jnp.where(n == k - 1, y[k - 1][a], up_in[a]) for a in range(NV)]
        return low_in, up_in

    halves = [entering(v) for v in range(2)]
    starts = [
        tuple(jnp.concatenate([halves[0][side][a], halves[1][side][a]], axis=0) for a in range(NV))
        for side in range(2)
    ]
    steps(norm_low, starts[0])

    def last_up(j, carry):
        carry = norm_up(j, carry)
        for a in range(NV):
            out[a, pl.ds(j, STEPS, stride=STEPS)] = carry[a]
        return carry

    steps(last_up, starts[1], reverse=True)

    to_next.wait_send()
    to_prev.wait_send()
    to_side.wait_send()
    pl.when(has_up)(to_up.wait_send)
    pl.when(has_down)(to_down.wait_send)

    def sent(j):
        @pl.when(2 * j != c)
        def _():
            to_owner(w_own, w_all, w_send, w_recv, j).wait_send()
            to_owner(b_own, b_all, b_send, b_recv, j).wait_send()

    each(OWNERS, sent)

    @pl.when(owner)
    def _():
        def returned(k):
            @pl.when(k != c)
            def _():
                to_segment(k).wait_send()

        each(CIRC, returned)

    for d in range(1, NORM):
        over_norm(d, rn, rn_send, rn_recv).wait_send()
        pl.when(n < NORM - 1)(over_norm(d, bl, bl_send, bl_recv).wait_send)
        pl.when(lax.rem(n + d, NORM) < n)(over_norm(d, bu, bu_send, bu_recv).wait_send)


def per_device(
    state, viscosity, visc_matrix, circ_lower_coef, circ_upper_coef, normal_lower_coef,
    normal_upper_coef, circ_plus, circ_minus, normal_plus, normal_minus,
):
    f32 = jnp.float32

    def vmem(*shape):
        return pltpu.VMEM(shape, f32)

    plane = (STEPS, LANES)
    block = (STEPS, STEPS, LANES)
    mats = NV * NV
    dma = pltpu.SemaphoreType.DMA
    scratch = [
        vmem(NV, STEPS + 2, 24, LANES),
        *[vmem(*block) for _ in range(5)],
        vmem(NV, *block), vmem(NV, *block),
        vmem(NV, STEPS * STEPS, LANES), vmem(NV, *block),
        vmem(2, *plane), vmem(2, *plane),
        vmem(18, *plane), vmem(2 * NV, *plane),
        vmem(18, CIRC, LANES), vmem(2 * NV, CIRC, LANES),
        vmem(2 * NV, CIRC, LANES), vmem(2 * NV, *plane),
        vmem(10, mats, 8, LANES),
        vmem(mats, *plane), vmem(mats, *plane),
        vmem(12, mats, 8, LANES), vmem(mats, CIRC, LANES),
        vmem(5, CIRC, LANES), vmem(5, CIRC, LANES),
        vmem(mats, 8, LANES), vmem(mats, 8, LANES), vmem(2, mats, 8, LANES),
        vmem(*block), vmem(NORM, mats + 2, *plane), vmem(2, NORM, NV, *plane),
        dma((4,)), dma((STEPS,)), dma((STEPS,)), dma((3,)),
        dma((5,)), dma((5,)),
        dma((OWNERS,)), dma((CIRC,)), dma((OWNERS,)), dma((CIRC,)),
        dma((CIRC,)), dma((OWNERS,)),
        *[dma((NORM,)) for _ in range(6)],
    ]
    anywhere = pl.BlockSpec(memory_space=pl.ANY)
    small = pl.BlockSpec(memory_space=pltpu.SMEM)
    flat = pl.pallas_call(
        kernel,
        out_shape=jax.ShapeDtypeStruct((NV, STEPS * STEPS, LANES), f32),
        in_specs=[anywhere] * 6 + [small] * 5,
        out_specs=pl.BlockSpec(memory_space=pltpu.VMEM),
        scratch_shapes=scratch,
        compiler_params=pltpu.CompilerParams(
            collective_id=0, has_side_effects=True, vmem_limit_bytes=32 * 1024 * 1024
        ),
    )(
        state, viscosity, circ_lower_coef, circ_upper_coef, normal_lower_coef, normal_upper_coef,
        visc_matrix, circ_plus, circ_minus, normal_plus, normal_minus,
    )
    return flat.reshape(NV, STEPS, STEPS, LANES)


def solution(mesh):
    placed = (
        P(None, "circ", "norm", "span"),
        P("circ", "norm", "span"),
        P(),
        P("circ", "norm", "span"),
        P("circ", "norm", "span"),
        P("circ", "norm", "span"),
        P("circ", "norm", "span"),
        P(),
        P(),
        P(),
        P(),
    )
    return jax.shard_map(
        per_device,
        mesh=mesh,
        in_specs=placed,
        out_specs=P(None, "circ", "norm", "span"),
        check_vma=False,
    )
```

time: 734 us -> 51.3 us (0.07); the launches traced: 720 us -> 50.9 us
  blocking collectives: 484 us -> 0 us
  local copies, waits for them, and re-layouts: 103 us -> 9.88 us
  matrix products: 52.9 us -> 0 us
  other arithmetic: 45.6 us -> 0 us
  Pallas kernels: 0 us -> 41 us
  between operations: 14 us -> 0.02 us
  starting transfers between devices: 11.2 us -> 0 us
  loops' own time: 7.64 us -> 0 us
    psum x2 -> x0, blocking collectives: 249 us -> none  [spread(): return lax.psum(block, axis)]
    all_gather x10 -> x0, blocking collectives: 235 us -> none  [prefix_2(): everything = jax.tree.map(lambda part: lax.all_gather(part, axis), array)]
    dot_general x291 -> x0, matrix products: 52.9 us -> none  [the longest x205 41.4 us: apply_matrix(): return jnp.einsum('ab,bxy->axy', mat, vec, precision=lax.Precision.HIGHEST)]
    dynamic_slice x72 -> x0, local copies, waits for them, and re-layouts: 50.5 us -> none  [hop(): new = combine(before, jax.tree.map(lambda part: part[at], everything))]
    unnamed x14 -> x0, other arithmetic: 43.6 us -> none
    pallas_call x0 -> x1, Pallas kernels: none -> 41 us  [per_device(): pl.pallas_call(kernel, out_shape=jax.ShapeDtypeStruct((NV, STEPS * STEPS,...]
    dynamic_update_slice x32 -> x0, local copies, waits for them, and re-layouts: 36.3 us -> none  [sweep(): last, values = lax.scan(step, start, items, reverse=backward)]
    ppermute x6 -> x0, starting transfers between devices: 11.2 us -> none  [the longest x3 9.42 us: padded(): lax.ppermute(lax.slice_in_dim(block, block.shape[dim] - width, None, axis...]
  transfers between devices with their start and end apart: 8 -> 0, of which waited for: 2 -> 0; matrix products, arithmetic and copies ran while one was open for 1% -> 0% of each run, Pallas kernels for 0% -> 0%
where the time goes in v1:
time: 51.3 us; the launch traced here: 50.9 us
  Pallas kernels  41 us (80%)
  local copies, waits for them, and re-layouts  9.88 us (19%)
    pallas_call x1, Pallas kernels, per_device(): pl.pallas_call(kernel, out_shape=jax.ShapeDtypeStruct((NV, STEPS * STEPS,...  41 us
    unnamed x23, local copies, waits for them, and re-layouts  9.88 us

profile of v1, /device:TPU:1, one launch (start us, length us, event | category | flops | bytes accessed | tf_op | source)
XLA Modules:
  0.0 50.9 jit_solution(7456188690715116965)
XLA Ops:
  0.0 0.0 copy-start
  0.0 1.1 %copy-done = f32[5,16,16,128]{3,2,1,0:T(8,128)S(1)} copy-done((f32[5,16,16,128]{3,2,1,0:T(8,128)S(1)}, f32[5,16,16,128]{3,2,1,0:T(8,128)}, u32[]{:S(2)}) %copy-start) | copy-done | bytes 655384
  1.1 0.0 copy-start.1
  1.1 0.9 %copy-done.1 = f32[16,16,128]{2,1,0:T(8,128)S(1)} copy-done((f32[16,16,128]{2,1,0:T(8,128)S(1)}, f32[16,16,128]{2,1,0:T(8,128)}, u32[]{:S(2)}) %copy-start.1) | copy-done | bytes 131096
  2.0 0.0 copy-start.2
  2.0 0.9 %copy-done.2 = f32[16,16,128]{2,1,0:T(8,128)S(1)} copy-done((f32[16,16,128]{2,1,0:T(8,128)S(1)}, f32[16,16,128]{2,1,0:T(8,128)}, u32[]{:S(2)}) %copy-start.2) | copy-done | bytes 131096
  2.9 0.0 copy-start.3
  2.9 0.9 %copy-done.3 = f32[16,16,128]{2,1,0:T(8,128)S(1)} copy-done((f32[16,16,128]{2,1,0:T(8,128)S(1)}, f32[16,16,128]{2,1,0:T(8,128)}, u32[]{:S(2)}) %copy-start.3) | copy-done | bytes 131096
  3.8 0.0 copy-start.4
  3.8 0.9 %copy-done.4 = f32[16,16,128]{2,1,0:T(8,128)S(1)} copy-done((f32[16,16,128]{2,1,0:T(8,128)S(1)}, f32[16,16,128]{2,1,0:T(8,128)}, u32[]{:S(2)}) %copy-start.4) | copy-done | bytes 131096
  4.7 0.0 copy-start.5
  4.7 0.9 %copy-done.5 = f32[16,16,128]{2,1,0:T(8,128)S(1)} copy-done((f32[16,16,128]{2,1,0:T(8,128)S(1)}, f32[16,16,128]{2,1,0:T(8,128)}, u32[]{:S(2)}) %copy-start.5) | copy-done | bytes 131096
  5.6 0.0 copy-start.6
  5.6 0.7 %copy-done.6 = f32[5,5]{1,0:T(8,128)S(1)} copy-done((f32[5,5]{1,0:T(8,128)S(1)}, f32[5,5]{1,0:T(8,128)}, u32[]{:S(2)}) %copy-start.6) | copy-done | bytes 124
  6.3 0.0 copy-start.7
  6.3 0.7 %copy-done.7 = f32[5,5]{1,0:T(8,128)S(1)} copy-done((f32[5,5]{1,0:T(8,128)S(1)}, f32[5,5]{1,0:T(8,128)}, u32[]{:S(2)}) %copy-start.7) | copy-done | bytes 124
  7.0 0.0 copy-start.8
  7.0 0.7 %copy-done.8 = f32[5,5]{1,0:T(8,128)S(1)} copy-done((f32[5,5]{1,0:T(8,128)S(1)}, f32[5,5]{1,0:T(8,128)}, u32[]{:S(2)}) %copy-start.8) | copy-done | bytes 124
  7.7 0.0 copy-start.9
  7.7 0.7 %copy-done.9 = f32[5,5]{1,0:T(8,128)S(1)} copy-done((f32[5,5]{1,0:T(8,128)S(1)}, f32[5,5]{1,0:T(8,128)}, u32[]{:S(2)}) %copy-start.9) | copy-done | bytes 124
  8.4 0.0 copy-start.10
  8.4 0.7 %copy-done.10 = f32[5,5]{1,0:T(8,128)S(1)} copy-done((f32[5,5]{1,0:T(8,128)S(1)}, f32[5,5]{1,0:T(8,128)}, u32[]{:S(2)}) %copy-start.10) | copy-done | bytes 124
  9.0 41.0 %shard_map.109 = f32[5,256,128]{2,1,0:T(8,128)S(1)} custom-call(f32[5,16,16,128]{3,2,1,0:T(8,128)S(1)} %copy-done, f32[16,16,128]{2,1,0:T(8,128)S(1)} %copy-done.1, f32[16,16,128]{2,1,0:T(8,128)S(1)} %copy-done.2, f32[16,16,128]{2,1,0:T(8,128)S(1)} %copy-done.3, f32[16,16,128]{2,1,0:T(8,128)S(1)} %copy-done.4, f32[16,16,128]{2,1,0:T(8,128)S(1)} %copy-done.5, ...), custom_call_target="tpu_custom_call" | custom-call | tf_op jit(solution)/shard_map/pallas_call | solution.py:630
  50.1 0.8 %copy.13 = f32[5,16,16,128]{3,2,1,0:T(8,128)} copy(f32[5,16,16,128]{3,2,1,0:T(8,128)S(1)} %bitcast.1) | data formatting | bytes 1310720
Async XLA Ops:
  0.0 1.1 %copy-start = (f32[5,16,16,128]{3,2,1,0:T(8,128)S(1)}, f32[5,16,16,128]{3,2,1,0:T(8,128)}, u32[]{:S(2)}) copy-start(f32[5,16,16,128]{3,2,1,0:T(8,128)} %state.1) | copy-start | bytes 1966084
  1.1 0.9 %copy-start.1 = (f32[16,16,128]{2,1,0:T(8,128)S(1)}, f32[16,16,128]{2,1,0:T(8,128)}, u32[]{:S(2)}) copy-start(f32[16,16,128]{2,1,0:T(8,128)} %visc_in.1) | copy-start | bytes 393220
  2.0 0.9 %copy-start.2 = (f32[16,16,128]{2,1,0:T(8,128)S(1)}, f32[16,16,128]{2,1,0:T(8,128)}, u32[]{:S(2)}) copy-start(f32[16,16,128]{2,1,0:T(8,128)} %cl_in.1) | copy-start | bytes 393220
  2.9 0.9 %copy-start.3 = (f32[16,16,128]{2,1,0:T(8,128)S(1)}, f32[16,16,128]{2,1,0:T(8,128)}, u32[]{:S(2)}) copy-start(f32[16,16,128]{2,1,0:T(8,128)} %cu_in.1) | copy-start | bytes 393220
  3.8 0.9 %copy-start.4 = (f32[16,16,128]{2,1,0:T(8,128)S(1)}, f32[16,16,128]{2,1,0:T(8,128)}, u32[]{:S(2)}) copy-start(f32[16,16,128]{2,1,0:T(8,128)} %nl_in.1) | copy-start | bytes 393220
  4.7 0.9 %copy-start.5 = (f32[16,16,128]{2,1,0:T(8,128)S(1)}, f32[16,16,128]{2,1,0:T(8,128)}, u32[]{:S(2)}) copy-start(f32[16,16,128]{2,1,0:T(8,128)} %nu_in.1) | copy-start | bytes 393220
  5.6 0.7 %copy-start.6 = (f32[5,5]{1,0:T(8,128)S(1)}, f32[5,5]{1,0:T(8,128)}, u32[]{:S(2)}) copy-start(f32[5,5]{1,0:T(8,128)} %vm_in.1) | copy-start | bytes 304
  6.3 0.7 %copy-start.7 = (f32[5,5]{1,0:T(8,128)S(1)}, f32[5,5]{1,0:T(8,128)}, u32[]{:S(2)}) copy-start(f32[5,5]{1,0:T(8,128)} %cp_in.1) | copy-start | bytes 304
  7.0 0.7 %copy-start.8 = (f32[5,5]{1,0:T(8,128)S(1)}, f32[5,5]{1,0:T(8,128)}, u32[]{:S(2)}) copy-start(f32[5,5]{1,0:T(8,128)} %cm_in.1) | copy-start | bytes 304
  7.7 0.7 %copy-start.9 = (f32[5,5]{1,0:T(8,128)S(1)}, f32[5,5]{1,0:T(8,128)}, u32[]{:S(2)}) copy-start(f32[5,5]{1,0:T(8,128)} %np_in.1) | copy-start | bytes 304
  8.4 0.7 %copy-start.10 = (f32[5,5]{1,0:T(8,128)S(1)}, f32[5,5]{1,0:T(8,128)}, u32[]{:S(2)}) copy-start(f32[5,5]{1,0:T(8,128)} %nm_in.1) | copy-start | bytes 304

commit v2 on v1

--- a/solution.py
+++ b/solution.py
@@ -11,7 +11,8 @@
 STEPS = 16
 LANES = 128
 OWNERS = 16
-STEP_UNROLL = 2
+STEP_UNROLL = 8
+SEND_UNROLL = 2
 
 
 def place(seg):
@@ -85,6 +86,17 @@
     return lax.fori_loop(0, STEPS // STEP_UNROLL, several, start)
 
 
+def far_first(count, me, body):
+    def some(t, carry):
+        for u in range(SEND_UNROLL // 2):
+            d = t * (SEND_UNROLL // 2) + u
+            body(lax.rem(me + count // 2 + d, count))
+            body(lax.rem(me + count // 2 + count - 1 - d, count))
+        return carry
+
+    lax.fori_loop(0, count // SEND_UNROLL, some, 0)
+
+
 def each(count, body):
     def one(k, carry):
         body(k)
@@ -94,13 +106,15 @@
 
 
 def kernel(
-    state, visc_in, cl_in, cu_in, nl_in, nu_in, vm_in, cp_in, cm_in, np_in, nm_in,
+    state, visc_in, cl_in, cu_in, nl_in, nu_in, vm_hbm, cp_hbm, cm_hbm, np_hbm, nm_hbm,
     out,
+    vm_in, cp_in, cm_in, np_in, nm_in, mat_sem,
     field, visc, cl, cu, nl, nu, rhs, low, turned, low_t,
-    edge, edge_in, w_own, b_own, w_all, b_all, back, back_in,
+    edge, edge_in, w_own, l_own, u_own, w_all, l_all, u_all, x_out, y_out, x_in, y_in,
     power, k_circ, k_norm, level, r_circ, a_low, a_up, g_low, g_up, m_norm, w_norm, rn, bn,
-    load_sem, tl_sem, tu_sem, self_sem,
-    halo_send, halo_recv, w_send, w_recv, b_send, b_recv, p_send, p_recv,
+    load_sem, tl_sem, tu_sem,
+    halo_send, halo_recv, w_send, w_recv, l_send, l_recv, u_send, u_recv,
+    x_send, x_recv, y_send, y_recv,
     rn_send, rn_recv, bl_send, bl_recv, bu_send, bu_recv,
 ):
     c, n, s = lax.axis_index("circ"), lax.axis_index("norm"), lax.axis_index("span")
@@ -116,19 +130,20 @@
 
     barrier = pltpu.get_barrier_semaphore()
 
-    def greet(d):
-        to = lax.rem(c + d + 1, CIRC)
-
-        @pl.when(jnp.logical_or(owner, lax.rem(to, 2) == 0))
+    def greet(to):
+        @pl.when(jnp.logical_or(jnp.logical_or(owner, to == c), lax.rem(to, 2) == 0))
         def _():
-            pl.semaphore_signal(barrier, inc=1, device_id=(to, n, s), device_id_type=MESH)
-
-    each(CIRC - 1, greet)
+            pl.semaphore_signal(barrier, inc=1, device_id=(to, n, 1 - s), device_id_type=MESH)
+
+    for d in (1, CIRC - 1):
+        pl.semaphore_signal(
+            barrier, inc=1, device_id=(lax.rem(c + d, CIRC), n, s), device_id_type=MESH
+        )
     for d in range(1, NORM):
         pl.semaphore_signal(
             barrier, inc=1, device_id=(c, lax.rem(n + d, NORM), s), device_id_type=MESH
         )
-    pl.semaphore_signal(barrier, inc=1, device_id=(c, n, 1 - s), device_id_type=MESH)
+    each(CIRC, greet)
 
     inside = pltpu.make_async_copy(
         state, field.at[:, pl.ds(1, STEPS), pl.ds(0, STEPS)], load_sem.at[0]
@@ -137,12 +152,18 @@
         pltpu.make_async_copy(src, dst, load_sem.at[1 + k])
         for k, (src, dst) in enumerate(((cl_in, cl), (cu_in, cu), (visc_in, visc)))
     ]
+    mats = [
+        pltpu.make_async_copy(src, dst, mat_sem.at[k])
+        for k, (src, dst) in enumerate(
+            zip((vm_hbm, cp_hbm, cm_hbm, np_hbm, nm_hbm), (vm_in, cp_in, cm_in, np_in, nm_in))
+        )
+    ]
     inside.start()
-    for copy in loads:
+    for copy in mats + loads:
         copy.start()
 
     def turn(src, dst, sem, j):
-        return pltpu.make_async_copy(src.at[:, j], dst.at[j], sem.at[j])
+        return pltpu.make_async_copy(src.at[:, j], dst.at[j], sem.at[0])
 
     def fetch(j):
         turn(nl_in, nl, tl_sem, j).start()
@@ -150,6 +171,102 @@
 
     each(STEPS, fetch)
 
+    inside.wait()
+    lane = lax.broadcasted_iota(jnp.int32, (STEPS, LANES), 1)
+
+    def slot(a, i):
+        return (0, a * STEPS + i) if a < 4 else (1, i)
+
+    def pack(i, packs):
+        packs = list(packs)
+        for a in range(NV):
+            g, k = slot(a, i)
+            mine = lax.rem(lane - 2 * k + 1 + LANES, LANES) <= 1
+            moved = pltpu.roll(field[a, i + 1, pl.ds(0, STEPS)], 2 * k, axis=1)
+            packs[g] = jnp.where(mine, moved, packs[g])
+        return tuple(packs)
+
+    packs = steps(pack, (zero, zero))
+    for g in range(2):
+        edge[g] = jnp.where(lane % 2 == 1, pltpu.roll(packs[g], 2, axis=1), packs[g])
+
+    pl.semaphore_wait(barrier, jnp.where(owner, CIRC, OWNERS + 1) + 2 + NORM - 1)
+
+    to_next = remote(
+        field.at[:, STEPS, pl.ds(0, STEPS)], field.at[:, 0, pl.ds(0, STEPS)],
+        halo_send.at[0], halo_recv.at[0], (lax.rem(c + 1, CIRC), n, s),
+    )
+    to_prev = remote(
+        field.at[:, 1, pl.ds(0, STEPS)], field.at[:, STEPS + 1, pl.ds(0, STEPS)],
+        halo_send.at[1], halo_recv.at[1], (lax.rem(c + CIRC - 1, CIRC), n, s),
+    )
+    to_side = remote(edge, edge_in, halo_send.at[2], halo_recv.at[2], (c, n, 1 - s))
+    to_up = remote(
+        field.at[:, pl.ds(1, STEPS), STEPS - 1], field.at[:, pl.ds(1, STEPS), 23],
+        halo_send.at[3], halo_recv.at[3], (c, n + 1, s),
+    )
+    to_down = remote(
+        field.at[:, pl.ds(1, STEPS), 0], field.at[:, pl.ds(1, STEPS), STEPS],
+        halo_send.at[4], halo_recv.at[4], (c, n - 1, s),
+    )
+    has_up, has_down = n < NORM - 1, n > 0
+    to_next.start()
+    to_prev.start()
+    to_side.start()
+    pl.when(has_up)(to_up.start)
+    pl.when(has_down)(to_down.start)
+
+    def nothing_at(at):
+        def fill(i, carry):
+            for a in range(NV):
+                field[a, i + 1, pl.ds(at, 1)] = jnp.zeros((1, LANES), jnp.float32)
+            return carry
+
+        steps(fill, 0)
+
+    pl.when(jnp.logical_not(has_up))(lambda: nothing_at(STEPS))
+    pl.when(jnp.logical_not(has_down))(lambda: nothing_at(23))
+
+    for copy in loads:
+        copy.wait()
+
+    def circ_scales(i, carry):
+        p, q = carry
+        p = p * cl[i]
+        w_own[2 + i] = q * p
+        return p, q * cu[i]
+
+    p, q = steps(circ_scales, (one, one))
+    w_own[0] = p
+    w_own[1] = q
+
+    def hand_in(src, dst, send, recv):
+        far_first(OWNERS, row, lambda j: remote(
+            src.at[:, j], dst.at[:, place(c)], send.at[0], recv.at[0], (2 * j, n, 1 - s)
+        ).start())
+
+    def give_back(src, dst, send, recv):
+        far_first(CIRC, c, lambda k: remote(
+            src.at[:, place(k)], dst.at[:, row], send.at[0], recv.at[0], (k, n, 1 - s)
+        ).start())
+
+    def whole(src, dst, send, recv):
+        out_of = remote(src, src, send.at[0], recv.at[0], (c, n, 1 - s))
+        into = remote(dst, dst, send.at[0], recv.at[0], (c, n, 1 - s))
+        return out_of.wait_send, into.wait_recv
+
+    def collected(*which):
+        whole(*which)[1]()
+
+    w_way = (w_own, w_all, w_send, w_recv)
+    l_way = (l_own, l_all, l_send, l_recv)
+    u_way = (u_own, u_all, u_send, u_recv)
+    x_way = (x_out, x_in, x_send, x_recv)
+    y_way = (y_out, y_in, y_send, y_recv)
+    hand_in(*w_way)
+
+    for copy in mats:
+        copy.wait()
     lane8 = lax.broadcasted_iota(jnp.int32, (8, LANES), 1)
     sub8 = lax.broadcasted_iota(jnp.int32, (8, LANES), 0)
     group = lane8 // 32
@@ -212,137 +329,6 @@
                     total = total + w[i] * table[e, pl.ds(i, 1)]
                 store(e, v, total)
 
-    for copy in loads:
-        copy.wait()
-
-    def circ_scales(i, carry):
-        p, q = carry
-        p = p * cl[i]
-        w_own[2 + i] = q * p
-        return p, q * cu[i]
-
-    p, q = steps(circ_scales, (one, one))
-    w_own[0] = p
-    w_own[1] = q
-
-    inside.wait()
-    lane = lax.broadcasted_iota(jnp.int32, (STEPS, LANES), 1)
-
-    def slot(a, i):
-        return (0, a * STEPS + i) if a < 4 else (1, i)
-
-    def pack(i, packs):
-        packs = list(packs)
-        for a in range(NV):
-            g, k = slot(a, i)
-            mine = lax.rem(lane - 2 * k + 1 + LANES, LANES) <= 1
-            moved = pltpu.roll(field[a, i + 1, pl.ds(0, STEPS)], 2 * k, axis=1)
-            packs[g] = jnp.where(mine, moved, packs[g])
-        return tuple(packs)
-
-    packs = steps(pack, (zero, zero))
-    for g in range(2):
-        edge[g] = jnp.where(lane % 2 == 1, pltpu.roll(packs[g], 2, axis=1), packs[g])
-
-    pl.semaphore_wait(barrier, jnp.where(owner, CIRC - 1, OWNERS) + NORM)
-
-    to_next = remote(
-        field.at[:, STEPS, pl.ds(0, STEPS)], field.at[:, 0, pl.ds(0, STEPS)],
-        halo_send.at[0], halo_recv.at[0], (lax.rem(c + 1, CIRC), n, s),
-    )
-    to_prev = remote(
-        field.at[:, 1, pl.ds(0, STEPS)], field.at[:, STEPS + 1, pl.ds(0, STEPS)],
-        halo_send.at[1], halo_recv.at[1], (lax.rem(c + CIRC - 1, CIRC), n, s),
-    )
-    to_side = remote(edge, edge_in, halo_send.at[2], halo_recv.at[2], (c, n, 1 - s))
-    to_up = remote(
-        field.at[:, pl.ds(1, STEPS), STEPS - 1], field.at[:, pl.ds(1, STEPS), 23],
-        halo_send.at[3], halo_recv.at[3], (c, n + 1, s),
-    )
-    to_down = remote(
-        field.at[:, pl.ds(1, STEPS), 0], field.at[:, pl.ds(1, STEPS), STEPS],
-        halo_send.at[4], halo_recv.at[4], (c, n - 1, s),
-    )
-    has_up, has_down = n < NORM - 1, n > 0
-    to_next.start()
-    to_prev.start()
-    to_side.start()
-    pl.when(has_up)(to_up.start)
-    pl.when(has_down)(to_down.start)
-
-    def nothing_at(at):
-        def fill(i, carry):
-            for a in range(NV):
-                field[a, i + 1, pl.ds(at, 1)] = jnp.zeros((1, LANES), jnp.float32)
-            return carry
-
-        steps(fill, 0)
-
-    pl.when(jnp.logical_not(has_up))(lambda: nothing_at(STEPS))
-    pl.when(jnp.logical_not(has_down))(lambda: nothing_at(23))
-
-    def to_owner(src, dst, send, recv, j):
-        return remote(
-            src.at[:, j], dst.at[:, place(c)], send.at[j], recv.at[c], (2 * j, n, s)
-        )
-
-    def from_segment(src, dst, send, recv, k):
-        return remote(src.at[:, 0], dst.at[:, place(k)], send.at[0], recv.at[k], (c, n, s))
-
-    def hand_in(src, dst, send, recv, k):
-        def one_row(j):
-            @pl.when(2 * j != c)
-            def _():
-                to_owner(src, dst, send, recv, j).start()
-
-        each(OWNERS, one_row)
-
-        @pl.when(owner)
-        def _():
-            pltpu.make_async_copy(src.at[:, row], dst.at[:, place(c)], self_sem.at[k]).start()
-
-    def collected(src, dst, send, recv, k):
-        def one_segment(seg):
-            @pl.when(seg != c)
-            def _():
-                from_segment(src, dst, send, recv, seg).wait_recv()
-
-        each(CIRC, one_segment)
-        pltpu.make_async_copy(src.at[:, row], dst.at[:, place(c)], self_sem.at[k]).wait()
-
-    hand_in(w_own, w_all, w_send, w_recv, 0)
-
-    def fetched(j):
-        turn(nl_in, nl, tl_sem, j).wait()
-        turn(nu_in, nu, tu_sem, j).wait()
-
-    each(STEPS, fetched)
-
-    def norm_scales(j, carry):
-        p, q = carry
-        p = p * nl[j]
-        w_norm[j] = q * p
-        return p, q * nu[j]
-
-    p, q = steps(norm_scales, (one, one))
-    rn[n, 0] = p
-    rn[n, 1] = q
-
-    def keep_norm(e, v, total):
-        rn[n, 2 + e, pl.ds(8 * v, 8)] = total
-
-    responses(lambda j, v: w_norm[j, pl.ds(8 * v, 8)], 2, k_norm, keep_norm)
-
-    def over_norm(d, buf, send, recv):
-        to = lax.rem(n + d, NORM)
-        return remote(buf.at[n], buf.at[n], send.at[d], recv.at[n], (c, to, s))
-
-    def from_norm(d, buf, send, recv):
-        k = lax.rem(n + d, NORM)
-        return remote(buf.at[k], buf.at[k], send.at[d], recv.at[k], (c, k, s))
-
-    for d in range(1, NORM):
-        over_norm(d, rn, rn_send, rn_recv).start()
 
     to_next.wait_recv()
     to_prev.wait_recv()
@@ -380,15 +366,45 @@
     zeros = (zero,) * NV
     end = steps(first_low, zeros)
     for a in range(NV):
-        b_own[a] = end[a]
+        l_own[a] = end[a]
+    hand_in(*l_way)
 
     def first_up(i, carry):
         return sweep_step([low[a, i] for a in range(NV)], cu[i], cm, carry)
 
     end = steps(first_up, zeros, reverse=True)
     for a in range(NV):
-        b_own[NV + a] = end[a]
-    hand_in(b_own, b_all, b_send, b_recv, 1)
+        u_own[a] = end[a]
+    hand_in(*u_way)
+
+    pltpu.make_async_copy(nl_in, nl, tl_sem.at[0]).wait()
+    pltpu.make_async_copy(nu_in, nu, tu_sem.at[0]).wait()
+
+    def norm_scales(j, carry):
+        p, q = carry
+        p = p * nl[j]
+        w_norm[j] = q * p
+        return p, q * nu[j]
+
+    p, q = steps(norm_scales, (one, one))
+    rn[n, 0] = p
+    rn[n, 1] = q
+
+    def keep_norm(e, v, total):
+        rn[n, 2 + e, pl.ds(8 * v, 8)] = total
+
+    responses(lambda j, v: w_norm[j, pl.ds(8 * v, 8)], 2, k_norm, keep_norm)
+
+    def over_norm(d, buf, send, recv):
+        to = lax.rem(n + d, NORM)
+        return remote(buf.at[n], buf.at[n], send.at[d], recv.at[n], (c, to, s))
+
+    def from_norm(d, buf, send, recv):
+        k = lax.rem(n + d, NORM)
+        return remote(buf.at[k], buf.at[k], send.at[d], recv.at[k], (c, k, s))
+
+    for d in range(1, NORM):
+        over_norm(d, rn, rn_send, rn_recv).start()
 
     def quad(ref, *at):
         return [ref[(*at, pl.ds(8 * v, 8))] for v in range(4)]
@@ -396,17 +412,9 @@
     def table(ref, *at):
         return [[ref[(*at, NV * r + k)] for k in range(NV)] for r in range(NV)]
 
-    def to_segment(k):
-        return remote(
-            back.at[:, place(k)], back_in.at[:, row], p_send.at[k], p_recv.at[row], (k, n, s)
-        )
-
-    def from_owner(j):
-        return remote(back.at[:, 0], back_in.at[:, j], p_send.at[0], p_recv.at[j], (2 * j, n, s))
-
     @pl.when(owner)
     def _():
-        collected(w_own, w_all, w_send, w_recv, 0)
+        collected(*w_way)
 
         def keep_circ(e, v, total):
             r_circ[e, pl.ds(8 * v, 8)] = total
@@ -424,8 +432,6 @@
                 for k in range(NV):
                     inv[NV * r + k] = solved[r][k]
 
-        collected(b_own, b_all, b_send, b_recv, 1)
-
         def closed(shift, side, store, inv):
             for t in range(5):
                 beside = [shifted(x, 1 << t, side == 1) for x in shift]
@@ -439,11 +445,14 @@
             solved = [apply(mat, [shift[a][v] for a in range(NV)]) for v in range(4)]
             return [shifted([solved[v][a] for v in range(4)], 1, side == 1) for a in range(NV)]
 
-        enter = closed([quad(b_all, a) for a in range(NV)], 0, a_low, g_low)
+        collected(*l_way)
+        enter = closed([quad(l_all, a) for a in range(NV)], 0, a_low, g_low)
         for a in range(NV):
             for v in range(4):
-                back[a, pl.ds(8 * v, 8)] = enter[a][v]
-        shift = [quad(b_all, NV + a) for a in range(NV)]
+                x_out[a, pl.ds(8 * v, 8)] = enter[a][v]
+        give_back(*x_way)
+        collected(*u_way)
+        shift = [quad(u_all, a) for a in range(NV)]
         for r in range(NV):
             for k in range(NV):
                 response = quad(r_circ, NV * r + k)
@@ -451,24 +460,10 @@
         enter = closed(shift, 1, a_up, g_up)
         for a in range(NV):
             for v in range(4):
-                back[NV + a, pl.ds(8 * v, 8)] = enter[a][v]
-
-        def give(k):
-            @pl.when(k != c)
-            def _():
-                to_segment(k).start()
-
-        each(CIRC, give)
-        own = pltpu.make_async_copy(back.at[:, place(c)], back_in.at[:, row], self_sem.at[2])
-        own.start()
-        own.wait()
-
-    def given(j):
-        @pl.when(2 * j != c)
-        def _():
-            from_owner(j).wait_recv()
-
-    each(OWNERS, given)
+                y_out[a, pl.ds(8 * v, 8)] = enter[a][v]
+        give_back(*y_way)
+
+    collected(*x_way)
 
     def second_low(i, carry):
         carry = sweep_step([rhs[a, i] for a in range(NV)], cl[i], cp, carry)
@@ -476,7 +471,8 @@
             low[a, i] = carry[a]
         return carry
 
-    steps(second_low, tuple(back_in[a] for a in range(NV)))
+    steps(second_low, tuple(x_in[a] for a in range(NV)))
+    collected(*y_way)
 
     def second_up(i, carry):
         carry = sweep_step([low[a, i] for a in range(NV)], cu[i], cm, carry)
@@ -484,7 +480,7 @@
             turned[a, pl.ds(i, STEPS, stride=STEPS)] = carry[a]
         return carry
 
-    steps(second_up, tuple(back_in[NV + a] for a in range(NV)), reverse=True)
+    steps(second_up, tuple(y_in[a] for a in range(NV)), reverse=True)
 
     nplus, nminus = scalars(np_in), scalars(nm_in)
 
@@ -568,22 +564,13 @@
     pl.when(has_up)(to_up.wait_send)
     pl.when(has_down)(to_down.wait_send)
 
-    def sent(j):
-        @pl.when(2 * j != c)
-        def _():
-            to_owner(w_own, w_all, w_send, w_recv, j).wait_send()
-            to_owner(b_own, b_all, b_send, b_recv, j).wait_send()
-
-    each(OWNERS, sent)
+    for way in (w_way, l_way, u_way):
+        whole(*way)[0]()
 
     @pl.when(owner)
     def _():
-        def returned(k):
-            @pl.when(k != c)
-            def _():
-                to_segment(k).wait_send()
-
-        each(CIRC, returned)
+        for way in (x_way, y_way):
+            whole(*way)[0]()
 
     for d in range(1, NORM):
         over_norm(d, rn, rn_send, rn_recv).wait_send()
@@ -605,36 +592,35 @@
     mats = NV * NV
     dma = pltpu.SemaphoreType.DMA
     scratch = [
+        *[pltpu.SMEM((NV, NV), f32) for _ in range(5)], dma((5,)),
         vmem(NV, STEPS + 2, 24, LANES),
         *[vmem(*block) for _ in range(5)],
         vmem(NV, *block), vmem(NV, *block),
         vmem(NV, STEPS * STEPS, LANES), vmem(NV, *block),
         vmem(2, *plane), vmem(2, *plane),
-        vmem(18, *plane), vmem(2 * NV, *plane),
-        vmem(18, CIRC, LANES), vmem(2 * NV, CIRC, LANES),
-        vmem(2 * NV, CIRC, LANES), vmem(2 * NV, *plane),
+        vmem(18, *plane), vmem(NV, *plane), vmem(NV, *plane),
+        vmem(18, CIRC, LANES), vmem(NV, CIRC, LANES), vmem(NV, CIRC, LANES),
+        vmem(NV, CIRC, LANES), vmem(NV, CIRC, LANES), vmem(NV, *plane), vmem(NV, *plane),
         vmem(10, mats, 8, LANES),
         vmem(mats, *plane), vmem(mats, *plane),
         vmem(12, mats, 8, LANES), vmem(mats, CIRC, LANES),
         vmem(5, CIRC, LANES), vmem(5, CIRC, LANES),
         vmem(mats, 8, LANES), vmem(mats, 8, LANES), vmem(2, mats, 8, LANES),
         vmem(*block), vmem(NORM, mats + 2, *plane), vmem(2, NORM, NV, *plane),
-        dma((4,)), dma((STEPS,)), dma((STEPS,)), dma((3,)),
+        dma((4,)), dma((1,)), dma((1,)),
         dma((5,)), dma((5,)),
-        dma((OWNERS,)), dma((CIRC,)), dma((OWNERS,)), dma((CIRC,)),
-        dma((CIRC,)), dma((OWNERS,)),
+        *[dma((1,)) for _ in range(10)],
         *[dma((NORM,)) for _ in range(6)],
     ]
-    anywhere = pl.BlockSpec(memory_space=pl.ANY)
-    small = pl.BlockSpec(memory_space=pltpu.SMEM)
+    anywhere = pl.BlockSpec(memory_space=pltpu.HBM)
     flat = pl.pallas_call(
         kernel,
-        out_shape=jax.ShapeDtypeStruct((NV, STEPS * STEPS, LANES), f32),
-        in_specs=[anywhere] * 6 + [small] * 5,
+        out_shape=pltpu.VMEM((NV, STEPS * STEPS, LANES), f32),
+        in_specs=[anywhere] * 11,
         out_specs=pl.BlockSpec(memory_space=pltpu.VMEM),
         scratch_shapes=scratch,
         compiler_params=pltpu.CompilerParams(
-            collective_id=0, has_side_effects=True, vmem_limit_bytes=32 * 1024 * 1024
+            collective_id=0, has_side_effects=True, vmem_limit_bytes=60 * 1024 * 1024
         ),
     )(
         state, viscosity, circ_lower_coef, circ_upper_coef, normal_lower_coef, normal_upper_coef,

time: 51.3 us -> 36.2 us (0.71)
  local copies, waits for them, and re-layouts: 9.88 us -> 0.84 us
  Pallas kernels: 41 us -> 35.3 us
    unnamed x23 -> x1, local copies, waits for them, and re-layouts: 9.88 us -> 0.84 us
    pallas_call x1, Pallas kernels: 41 us -> 35.3 us  [per_device(): pl.pallas_call(kernel, out_shape=pltpu.VMEM((NV, STEPS * STEPS, LANES), f...]
where the time goes in v2:
time: 36.2 us; the launch traced here: 36.1 us
  Pallas kernels  35.3 us (98%)
  local copies, waits for them, and re-layouts  0.84 us (2%)
    pallas_call x1, Pallas kernels, per_device(): pl.pallas_call(kernel, out_shape=pltpu.VMEM((NV, STEPS * STEPS, LANES), f...  35.3 us
    unnamed x1, local copies, waits for them, and re-layouts  0.84 us

profile of v2, /device:TPU:1, one launch (start us, length us, event | category | flops | bytes accessed | tf_op | source)
XLA Modules:
  0.0 36.1 jit_solution(3855907972711967358)
XLA Ops:
  0.0 35.3 %shard_map.109 = f32[5,256,128]{2,1,0:T(8,128)S(1)} custom-call(f32[5,16,16,128]{3,2,1,0:T(8,128)} %state.1, f32[16,16,128]{2,1,0:T(8,128)} %visc_in.1, f32[16,16,128]{2,1,0:T(8,128)} %cl_in.1, f32[16,16,128]{2,1,0:T(8,128)} %cu_in.1, f32[16,16,128]{2,1,0:T(8,128)} %nl_in.1, f32[16,16,128]{2,1,0:T(8,128)} %nu_in.1, f32[5,5]{1,0:T(8,128)} %vm_hbm.1, ...), custom_call_target="tpu_custom_call" | custom-call | tf_op jit(solution)/shard_map/pallas_call | solution.py:616
  35.3 0.8 %copy.13 = f32[5,16,16,128]{3,2,1,0:T(8,128)} copy(f32[5,16,16,128]{3,2,1,0:T(8,128)S(1)} %bitcast.1) | data formatting | bytes 1310720

commit v3 on v2

--- a/solution.py
+++ b/solution.py
@@ -11,7 +11,7 @@
 STEPS = 16
 LANES = 128
 OWNERS = 16
-STEP_UNROLL = 8
+STEP_UNROLL = 16
 SEND_UNROLL = 2
 
 
@@ -30,13 +30,18 @@
     return [groups[v - d] if v >= d else turn(groups[v - d + 4], 1) for v in range(4)]
 
 
-def apply(mat, vec):
+def total(terms):
+    while len(terms) > 1:
+        pairs = [x + y for x, y in zip(terms[::2], terms[1::2])]
+        terms = pairs + terms[2 * len(pairs) :]
+    return terms[0]
+
+
+def apply(mat, vec, more=None):
     out = []
     for r in range(NV):
-        total = mat[r][0] * vec[0]
-        for c in range(1, NV):
-            total = total + mat[r][c] * vec[c]
-        out.append(total)
+        terms = [mat[r][c] * vec[c] for c in range(NV)]
+        out.append(total(terms if more is None else terms + [more[r]]))
     return out
 
 
@@ -44,18 +49,12 @@
     out = []
     for r in range(NV):
         for c in range(NV):
-            total = a[NV * r] * b[c]
-            for k in range(1, NV):
-                total = total + a[NV * r + k] * b[NV * k + c]
-            out.append(total)
+            out.append(total([a[NV * r + k] * b[NV * k + c] for k in range(NV)]))
     return out
 
 
-def inverse(scale, mat):
-    rows = [
-        [(1.0 if r == c else 0.0) - scale * mat[r][c] for c in range(NV)] for r in range(NV)
-    ]
-    inv = [[None] * NV for _ in range(NV)]
+def inverse(rows):
+    rows = [list(row) for row in rows]
     for k in range(NV):
         pivot = 1.0 / rows[k][k]
         for c in range(NV):
@@ -110,15 +109,17 @@
     out,
     vm_in, cp_in, cm_in, np_in, nm_in, mat_sem,
     field, visc, cl, cu, nl, nu, rhs, low, turned, low_t,
-    edge, edge_in, w_own, l_own, u_own, w_all, l_all, u_all, x_out, y_out, x_in, y_in,
-    power, k_circ, k_norm, level, r_circ, a_low, a_up, g_low, g_up, m_norm, w_norm, rn, bn,
+    edge, edge_in, before, after, wall_lo, wall_hi, wall_mix, side_mix, w_own, l_own, u_own, w_all, l_all, u_all, x_out, y_out, x_in, y_in,
+    power, k_circ, k_norm, level, r_circ, a_low, a_up, g_low, g_up,
+    m_norm, rs, wn, rn, bn,
     load_sem, tl_sem, tu_sem,
     halo_send, halo_recv, w_send, w_recv, l_send, l_recv, u_send, u_recv,
     x_send, x_recv, y_send, y_recv,
-    rn_send, rn_recv, bl_send, bl_recv, bu_send, bu_recv,
+    rs_send, rs_recv, wn_send, wn_recv, bl_send, bl_recv, bu_send, bu_recv,
 ):
     c, n, s = lax.axis_index("circ"), lax.axis_index("norm"), lax.axis_index("span")
     owner = lax.rem(c, 2) == 0
+    not_owner = lax.rem(c, 2) == 1
     row = c // 2
     zero = jnp.zeros((STEPS, LANES), jnp.float32)
     one = jnp.ones((STEPS, LANES), jnp.float32)
@@ -130,23 +131,25 @@
 
     barrier = pltpu.get_barrier_semaphore()
 
-    def greet(to):
-        @pl.when(jnp.logical_or(jnp.logical_or(owner, to == c), lax.rem(to, 2) == 0))
-        def _():
-            pl.semaphore_signal(barrier, inc=1, device_id=(to, n, 1 - s), device_id_type=MESH)
-
-    for d in (1, CIRC - 1):
-        pl.semaphore_signal(
-            barrier, inc=1, device_id=(lax.rem(c + d, CIRC), n, s), device_id_type=MESH
-        )
-    for d in range(1, NORM):
-        pl.semaphore_signal(
-            barrier, inc=1, device_id=(c, lax.rem(n + d, NORM), s), device_id_type=MESH
-        )
-    each(CIRC, greet)
+    def greet(*to):
+        pl.semaphore_signal(barrier, inc=1, device_id=to, device_id_type=MESH)
+
+    greet(c, n, 1 - s)
+    greet(lax.rem(c + 1, CIRC), n, s)
+    greet(lax.rem(c + CIRC - 1, CIRC), n, s)
+    for d in range(1, NORM):
+        greet(c, lax.rem(n + d, NORM), s)
+
+    @pl.when(owner)
+    def _():
+        each(CIRC - 1, lambda d: greet(lax.rem(c + d + 1, CIRC), n, 1 - s))
+
+    @pl.when(not_owner)
+    def _():
+        each(OWNERS, lambda j: greet(2 * j, n, 1 - s))
 
     inside = pltpu.make_async_copy(
-        state, field.at[:, pl.ds(1, STEPS), pl.ds(0, STEPS)], load_sem.at[0]
+        state, field.at[:, pl.ds(1, STEPS)], load_sem.at[0]
     )
     loads = [
         pltpu.make_async_copy(src, dst, load_sem.at[1 + k])
@@ -171,6 +174,12 @@
 
     each(STEPS, fetch)
 
+    to_next = remote(
+        field.at[:, STEPS], before, halo_send.at[3], halo_recv.at[3], (lax.rem(c + 1, CIRC), n, s)
+    )
+    to_prev = remote(
+        field.at[:, 1], after, halo_send.at[4], halo_recv.at[4], (lax.rem(c + CIRC - 1, CIRC), n, s)
+    )
     inside.wait()
     lane = lax.broadcasted_iota(jnp.int32, (STEPS, LANES), 1)
 
@@ -182,7 +191,7 @@
         for a in range(NV):
             g, k = slot(a, i)
             mine = lax.rem(lane - 2 * k + 1 + LANES, LANES) <= 1
-            moved = pltpu.roll(field[a, i + 1, pl.ds(0, STEPS)], 2 * k, axis=1)
+            moved = pltpu.roll(field[a, i + 1], 2 * k, axis=1)
             packs[g] = jnp.where(mine, moved, packs[g])
         return tuple(packs)
 
@@ -192,22 +201,12 @@
 
     pl.semaphore_wait(barrier, jnp.where(owner, CIRC, OWNERS + 1) + 2 + NORM - 1)
 
-    to_next = remote(
-        field.at[:, STEPS, pl.ds(0, STEPS)], field.at[:, 0, pl.ds(0, STEPS)],
-        halo_send.at[0], halo_recv.at[0], (lax.rem(c + 1, CIRC), n, s),
-    )
-    to_prev = remote(
-        field.at[:, 1, pl.ds(0, STEPS)], field.at[:, STEPS + 1, pl.ds(0, STEPS)],
-        halo_send.at[1], halo_recv.at[1], (lax.rem(c + CIRC - 1, CIRC), n, s),
-    )
-    to_side = remote(edge, edge_in, halo_send.at[2], halo_recv.at[2], (c, n, 1 - s))
+    to_side = remote(edge, edge_in, halo_send.at[0], halo_recv.at[0], (c, n, 1 - s))
     to_up = remote(
-        field.at[:, pl.ds(1, STEPS), STEPS - 1], field.at[:, pl.ds(1, STEPS), 23],
-        halo_send.at[3], halo_recv.at[3], (c, n + 1, s),
+        field.at[:, pl.ds(1, STEPS), STEPS - 1], wall_lo, halo_send.at[1], halo_recv.at[1], (c, n + 1, s)
     )
     to_down = remote(
-        field.at[:, pl.ds(1, STEPS), 0], field.at[:, pl.ds(1, STEPS), STEPS],
-        halo_send.at[4], halo_recv.at[4], (c, n - 1, s),
+        field.at[:, pl.ds(1, STEPS), 0], wall_hi, halo_send.at[2], halo_recv.at[2], (c, n - 1, s)
     )
     has_up, has_down = n < NORM - 1, n > 0
     to_next.start()
@@ -216,19 +215,16 @@
     pl.when(has_up)(to_up.start)
     pl.when(has_down)(to_down.start)
 
-    def nothing_at(at):
-        def fill(i, carry):
-            for a in range(NV):
-                field[a, i + 1, pl.ds(at, 1)] = jnp.zeros((1, LANES), jnp.float32)
-            return carry
-
-        steps(fill, 0)
-
-    pl.when(jnp.logical_not(has_up))(lambda: nothing_at(STEPS))
-    pl.when(jnp.logical_not(has_down))(lambda: nothing_at(23))
-
-    for copy in loads:
+    def clear(ref):
+        for a in range(NV):
+            ref[a] = zero
+
+    pl.when(n == NORM - 1)(lambda: clear(wall_hi))
+    pl.when(n == 0)(lambda: clear(wall_lo))
+
+    for copy in loads + mats:
         copy.wait()
+    vm, cp, cm = scalars(vm_in), scalars(cp_in), scalars(cm_in)
 
     def circ_scales(i, carry):
         p, q = carry
@@ -265,8 +261,114 @@
     y_way = (y_out, y_in, y_send, y_recv)
     hand_in(*w_way)
 
-    for copy in mats:
-        copy.wait()
+    pltpu.make_async_copy(nl_in, nl, tl_sem.at[0]).wait()
+    pltpu.make_async_copy(nu_in, nu, tu_sem.at[0]).wait()
+
+    def norm_scales(j, carry):
+        p, q = carry
+        p = p * nl[j]
+        wn[n, 1 + j] = q * p
+        return p, q * nu[j]
+
+    p, q = steps(norm_scales, (one, one))
+    rs[n] = p
+    wn[n, 0] = q
+
+    def over_norm(d, buf, send, recv):
+        to = lax.rem(n + d, NORM)
+        return remote(buf.at[n], buf.at[n], send.at[d], recv.at[n], (c, to, s))
+
+    def from_norm(d, buf, send, recv):
+        k = lax.rem(n + d, NORM)
+        return remote(buf.at[k], buf.at[k], send.at[d], recv.at[k], (c, k, s))
+
+    def scale_used(k):
+        return jnp.logical_and(k > 0, k < NORM - 1)
+
+    for d in range(1, NORM):
+        pl.when(scale_used(n))(over_norm(d, rs, rs_send, rs_recv).start)
+        pl.when(lax.rem(n + d, NORM) < n)(over_norm(d, wn, wn_send, wn_recv).start)
+
+    sub = lax.broadcasted_iota(jnp.int32, (STEPS, LANES), 0)
+    for a in range(NV):
+        field[a, 0] = zero
+        field[a, STEPS + 1] = zero
+
+    def inner(i, carry):
+        lap = []
+        for a in range(NV):
+            mid = field[a, i + 1]
+            below = jnp.where(sub == 0, 0.0, pltpu.roll(mid, 1, axis=0))
+            above = jnp.where(sub == STEPS - 1, 0.0, pltpu.roll(mid, STEPS - 1, axis=0))
+            left = jnp.where(lane == 0, 0.0, pltpu.roll(mid, 1, axis=1))
+            right = jnp.where(lane == LANES - 1, 0.0, pltpu.roll(mid, LANES - 1, axis=1))
+            around = field[a, i] + field[a, i + 2]
+            lap.append(around + (left + right) + (below + above) - 6.0 * mid)
+        mixed = apply(vm, lap)
+        for a in range(NV):
+            rhs[a, i] = visc[i] * mixed[a]
+        return carry
+
+    steps(inner, 0)
+
+    to_next.wait_recv()
+    to_prev.wait_recv()
+    to_side.wait_recv()
+    pl.when(has_up)(to_down.wait_recv)
+    pl.when(has_down)(to_up.wait_recv)
+
+    for k, ref in enumerate((wall_lo, wall_hi)):
+        mixed = apply(vm, [ref[a] for a in range(NV)])
+        for a in range(NV):
+            wall_mix[k, a] = mixed[a]
+    mixed = apply(
+        vm,
+        [edge_in[0]]
+        + [pltpu.roll(edge_in[0], LANES - 32 * a, axis=1) for a in range(1, 4)]
+        + [edge_in[1]],
+    )
+    for a in range(NV):
+        side_mix[a] = mixed[a]
+    for at, ref in ((0, before), (STEPS - 1, after)):
+        mixed = apply(vm, [ref[a] for a in range(NV)])
+        for a in range(NV):
+            rhs[a, at] = rhs[a, at] + visc[at] * mixed[a]
+    lane_half = lax.broadcasted_iota(jnp.int32, (8, LANES), 1)
+    sub_half = lax.broadcasted_iota(jnp.int32, (8, LANES), 0)
+    outer = jnp.logical_or(lane_half == 0, lane_half == LANES - 1)
+
+    def sweep_step(value, scale, mat, carry):
+        return tuple(apply(mat, [scale * x for x in carry], value))
+
+    def first_low(i, carry):
+        value = []
+        for a in range(NV):
+            beyond = pltpu.roll(side_mix[a], LANES - 1 - 2 * i, axis=1)
+            more = []
+            for h in range(2):
+                wall = jnp.where(sub_half == 7 * h, wall_mix[h, a, pl.ds(i, 1)], 0.0)
+                more.append(jnp.where(outer, beyond[8 * h : 8 * h + 8], 0.0) + wall)
+            value.append(rhs[a, i] + visc[i] * jnp.concatenate(more, axis=0))
+            rhs[a, i] = value[a]
+        carry = sweep_step(value, cl[i], cp, carry)
+        for a in range(NV):
+            low[a, i] = carry[a]
+        return carry
+
+    zeros = (zero,) * NV
+    end = steps(first_low, zeros)
+    for a in range(NV):
+        l_own[a] = end[a]
+    hand_in(*l_way)
+
+    def first_up(i, carry):
+        return sweep_step([low[a, i] for a in range(NV)], cu[i], cm, carry)
+
+    end = steps(first_up, zeros, reverse=True)
+    for a in range(NV):
+        u_own[a] = end[a]
+    hand_in(*u_way)
+
     lane8 = lax.broadcasted_iota(jnp.int32, (8, LANES), 1)
     sub8 = lax.broadcasted_iota(jnp.int32, (8, LANES), 0)
     group = lane8 // 32
@@ -324,87 +426,8 @@
         for v in range(count):
             w = [weight(i, v) for i in range(STEPS)]
             for e in range(NV * NV):
-                total = w[0] * table[e, pl.ds(0, 1)]
-                for i in range(1, STEPS):
-                    total = total + w[i] * table[e, pl.ds(i, 1)]
-                store(e, v, total)
-
-
-    to_next.wait_recv()
-    to_prev.wait_recv()
-    to_side.wait_recv()
-    pl.when(has_up)(to_down.wait_recv)
-    pl.when(has_down)(to_up.wait_recv)
-
-    vm, cp, cm = scalars(vm_in), scalars(cp_in), scalars(cm_in)
-
-    def sweep_step(value, scale, mat, carry):
-        moved = apply(mat, carry)
-        return tuple(value[a] + scale * moved[a] for a in range(NV))
-
-    def first_low(i, carry):
-        lap = []
-        for a in range(NV):
-            tall = field[a, i + 1]
-            mid = tall[:STEPS]
-            wall = pltpu.roll(tall, 1, axis=0)[:STEPS] + pltpu.roll(tall, 23, axis=0)[:STEPS]
-            g, k = slot(a, i)
-            beyond = pltpu.roll(edge_in[g], LANES - 1 - 2 * k, axis=1)
-            left = jnp.where(lane == 0, beyond, pltpu.roll(mid, 1, axis=1))
-            right = jnp.where(lane == LANES - 1, beyond, pltpu.roll(mid, LANES - 1, axis=1))
-            around = field[a, i, pl.ds(0, STEPS)] + field[a, i + 2, pl.ds(0, STEPS)]
-            lap.append(around + (left + right) + wall - 6.0 * mid)
-        mixed = apply(vm, lap)
-        value = [visc[i] * x for x in mixed]
-        for a in range(NV):
-            rhs[a, i] = value[a]
-        carry = sweep_step(value, cl[i], cp, carry)
-        for a in range(NV):
-            low[a, i] = carry[a]
-        return carry
-
-    zeros = (zero,) * NV
-    end = steps(first_low, zeros)
-    for a in range(NV):
-        l_own[a] = end[a]
-    hand_in(*l_way)
-
-    def first_up(i, carry):
-        return sweep_step([low[a, i] for a in range(NV)], cu[i], cm, carry)
-
-    end = steps(first_up, zeros, reverse=True)
-    for a in range(NV):
-        u_own[a] = end[a]
-    hand_in(*u_way)
-
-    pltpu.make_async_copy(nl_in, nl, tl_sem.at[0]).wait()
-    pltpu.make_async_copy(nu_in, nu, tu_sem.at[0]).wait()
-
-    def norm_scales(j, carry):
-        p, q = carry
-        p = p * nl[j]
-        w_norm[j] = q * p
-        return p, q * nu[j]
-
-    p, q = steps(norm_scales, (one, one))
-    rn[n, 0] = p
-    rn[n, 1] = q
-
-    def keep_norm(e, v, total):
-        rn[n, 2 + e, pl.ds(8 * v, 8)] = total
-
-    responses(lambda j, v: w_norm[j, pl.ds(8 * v, 8)], 2, k_norm, keep_norm)
-
-    def over_norm(d, buf, send, recv):
-        to = lax.rem(n + d, NORM)
-        return remote(buf.at[n], buf.at[n], send.at[d], recv.at[n], (c, to, s))
-
-    def from_norm(d, buf, send, recv):
-        k = lax.rem(n + d, NORM)
-        return remote(buf.at[k], buf.at[k], send.at[d], recv.at[k], (c, k, s))
-
-    for d in range(1, NORM):
-        over_norm(d, rn, rn_send, rn_recv).start()
+                store(e, v, total([w[i] * table[e, pl.ds(i, 1)] for i in range(STEPS)]))
+
 
     def quad(ref, *at):
         return [ref[(*at, pl.ds(8 * v, 8))] for v in range(4)]
@@ -427,7 +450,11 @@
                     store[t, pl.ds(8 * v, 8)] = scale[v]
                 beside = shifted(scale, 1 << t, side == 1)
                 scale = [scale[v] * beside[v] for v in range(4)]
-            solved = inverse(scale[0], table(level, 6 * side + 5))
+            whole_turn = table(level, 6 * side + 5)
+            solved = inverse([
+                [(1.0 if r == k else 0.0) - scale[0] * whole_turn[r][k] for k in range(NV)]
+                for r in range(NV)
+            ])
             for r in range(NV):
                 for k in range(NV):
                     inv[NV * r + k] = solved[r][k]
@@ -437,10 +464,15 @@
                 beside = [shifted(x, 1 << t, side == 1) for x in shift]
                 scale = quad(store, t)
                 mat = table(level, 6 * side + t)
-                moved = [apply(mat, [beside[a][v] for a in range(NV)]) for v in range(4)]
-                shift = [
-                    [shift[a][v] + scale[v] * moved[v][a] for v in range(4)] for a in range(NV)
+                moved = [
+                    apply(
+                        mat,
+                        [scale[v] * beside[a][v] for a in range(NV)],
+                        [shift[a][v] for a in range(NV)],
+                    )
+                    for v in range(4)
                 ]
+                shift = [[moved[v][a] for v in range(4)] for a in range(NV)]
             mat = table(inv)
             solved = [apply(mat, [shift[a][v] for a in range(NV)]) for v in range(4)]
             return [shifted([solved[v][a] for v in range(4)], 1, side == 1) for a in range(NV)]
@@ -463,6 +495,51 @@
                 y_out[a, pl.ds(8 * v, 8)] = enter[a][v]
         give_back(*y_way)
 
+    for d in range(1, NORM):
+        k = lax.rem(n + d, NORM)
+        pl.when(k > n)(from_norm(d, wn, wn_send, wn_recv).wait_recv)
+
+    def of_norm(k):
+        def keep_norm(e, v, total):
+            rn[k, e, pl.ds(8 * v, 8)] = total
+
+        @pl.when(k > n)
+        def _():
+            responses(lambda j, v: wn[k, 1 + j, pl.ds(8 * v, 8)], 2, k_norm, keep_norm)
+
+    each(NORM, of_norm)
+    for d in range(1, NORM):
+        k = lax.rem(n + d, NORM)
+        pl.when(scale_used(k))(from_norm(d, rs, rs_send, rs_recv).wait_recv)
+    plus_16, minus_16 = table(m_norm, 0), table(m_norm, 1)
+
+    def product(a, b):
+        return [
+            [total([a[r][k] * b[k][c] for k in range(NV)]) for c in range(NV)] for r in range(NV)
+        ]
+
+    def fold(k):
+        for v in range(2):
+            half = pl.ds(8 * v, 8)
+            beyond = [[rn[k + 1, NV * r + c, half] for c in range(NV)] for r in range(NV)]
+            moved = product(minus_16, [[wn[k, 0, half] * x for x in line] for line in beyond])
+
+            @pl.when(k == n)
+            def _():
+                for r in range(NV):
+                    for c in range(NV):
+                        rn[k, NV * r + c, half] = moved[r][c]
+
+            @pl.when(k > n)
+            def _():
+                both = product(moved, plus_16)
+                for r in range(NV):
+                    for c in range(NV):
+                        rn[k, NV * r + c, half] = rn[k, NV * r + c, half] + rs[k, half] * both[r][c]
+
+    for k in (2, 1):
+        pl.when(k >= n)(lambda k=k: fold(k))
+
     collected(*x_way)
 
     def second_low(i, carry):
@@ -501,54 +578,67 @@
     for a in range(NV):
         bn[0, n, a] = end[a]
     for d in range(1, NORM):
-        @pl.when(n < NORM - 1)
-        def _():
-            over_norm(d, bl, bl_send, bl_recv).start()
-
+        pl.when(lax.rem(n + d, NORM) > n)(over_norm(d, bl, bl_send, bl_recv).start)
+
+    below = end
     end = steps(norm_up, zeros, reverse=True)
-    for a in range(NV):
-        bn[1, n, a] = end[a]
-    for d in range(1, NORM):
-        @pl.when(lax.rem(n + d, NORM) < n)
-        def _():
-            over_norm(d, bu, bu_send, bu_recv).start()
+    for v in range(2):
+        half = pl.ds(8 * v, 8)
+        own = [[rn[n, NV * r + a, half] for a in range(NV)] for r in range(NV)]
+        added = apply(own, [x[8 * v : 8 * v + 8] for x in below])
+        for a in range(NV):
+            upper = end[a][8 * v : 8 * v + 8]
+            bn[1, n, a, half] = upper + jnp.where(scale_used(n), added[a], 0.0)
+    for d in range(1, NORM):
+        pl.when(lax.rem(n + d, NORM) < n)(over_norm(d, bu, bu_send, bu_recv).start)
 
     for d in range(1, NORM):
         k = lax.rem(n + d, NORM)
-        from_norm(d, rn, rn_send, rn_recv).wait_recv()
-        pl.when(k < NORM - 1)(from_norm(d, bl, bl_send, bl_recv).wait_recv)
-        pl.when(k > n)(from_norm(d, bu, bu_send, bu_recv).wait_recv)
-
-    def entering(v):
+        pl.when(k < n)(from_norm(d, bl, bl_send, bl_recv).wait_recv)
+
+    none = jnp.zeros((8, LANES), jnp.float32)
+
+    def joined(halves):
+        return tuple(
+            jnp.concatenate([halves[0][a], halves[1][a]], axis=0) for a in range(NV)
+        )
+
+    def chosen(by_place):
+        enter = [none] * NV
+        for k, value in by_place.items():
+            enter = [jnp.where(n == k, value[a], enter[a]) for a in range(NV)]
+        return enter
+
+    def entering_low(v):
         half = pl.ds(8 * v, 8)
-        plus, minus = table(m_norm, 0), table(m_norm, 1)
         x = {1: [bn[0, 0, a, half] for a in range(NV)]}
         for k in (1, 2):
-            moved = apply(plus, x[k])
-            x[k + 1] = [bn[0, k, a, half] + rn[k, 0, half] * moved[a] for a in range(NV)]
-        y = {}
-        for k in (3, 2, 1):
-            value = [bn[1, k, a, half] for a in range(NV)]
-            for r in range(NV):
-                for a in range(NV):
-                    value[r] = value[r] + rn[k, 2 + NV * r + a, half] * x[k][a]
-            if k < 3:
-                moved = apply(minus, y[k])
-                value = [value[a] + rn[k, 1, half] * moved[a] for a in range(NV)]
-            y[k - 1] = value
-        none = jnp.zeros((8, LANES), jnp.float32)
-        low_in, up_in = [none] * NV, [none] * NV
-        for k in (1, 2, 3):
-            low_in = [jnp.where(n == k, x[k][a], low_in[a]) for a in range(NV)]
-            up_in = [jnp.where(n == k - 1, y[k - 1][a], up_in[a]) for a in range(NV)]
-        return low_in, up_in
-
-    halves = [entering(v) for v in range(2)]
-    starts = [
-        tuple(jnp.concatenate([halves[0][side][a], halves[1][side][a]], axis=0) for a in range(NV))
-        for side in range(2)
-    ]
-    steps(norm_low, starts[0])
+            x[k + 1] = apply(
+                plus_16, [rs[k, half] * y for y in x[k]], [bn[0, k, a, half] for a in range(NV)]
+            )
+        return chosen(x)
+
+    start = joined([entering_low(v) for v in range(2)])
+    leave = steps(norm_low, start)
+
+    for d in range(1, NORM):
+        k = lax.rem(n + d, NORM)
+        pl.when(k > n)(from_norm(d, bu, bu_send, bu_recv).wait_recv)
+
+    after_me = lax.rem(n + 1, NORM)
+
+    def entering_up(v):
+        half = pl.ds(8 * v, 8)
+        y = {2: [bn[1, 3, a, half] for a in range(NV)]}
+        for k in (2, 1):
+            y[k - 1] = apply(
+                minus_16, [wn[k, 0, half] * z for z in y[k]], [bn[1, k, a, half] for a in range(NV)]
+            )
+        mat = [[rn[after_me, NV * r + a, half] for a in range(NV)] for r in range(NV)]
+        enter = apply(mat, [x[8 * v : 8 * v + 8] for x in leave], chosen(y))
+        return [jnp.where(n < NORM - 1, x, 0.0) for x in enter]
+
+    start = joined([entering_up(v) for v in range(2)])
 
     def last_up(j, carry):
         carry = norm_up(j, carry)
@@ -556,7 +646,7 @@
             out[a, pl.ds(j, STEPS, stride=STEPS)] = carry[a]
         return carry
 
-    steps(last_up, starts[1], reverse=True)
+    steps(last_up, start, reverse=True)
 
     to_next.wait_send()
     to_prev.wait_send()
@@ -573,8 +663,9 @@
             whole(*way)[0]()
 
     for d in range(1, NORM):
-        over_norm(d, rn, rn_send, rn_recv).wait_send()
-        pl.when(n < NORM - 1)(over_norm(d, bl, bl_send, bl_recv).wait_send)
+        pl.when(scale_used(n))(over_norm(d, rs, rs_send, rs_recv).wait_send)
+        pl.when(lax.rem(n + d, NORM) < n)(over_norm(d, wn, wn_send, wn_recv).wait_send)
+        pl.when(lax.rem(n + d, NORM) > n)(over_norm(d, bl, bl_send, bl_recv).wait_send)
         pl.when(lax.rem(n + d, NORM) < n)(over_norm(d, bu, bu_send, bu_recv).wait_send)
 
 
@@ -593,11 +684,13 @@
     dma = pltpu.SemaphoreType.DMA
     scratch = [
         *[pltpu.SMEM((NV, NV), f32) for _ in range(5)], dma((5,)),
-        vmem(NV, STEPS + 2, 24, LANES),
+        vmem(NV, STEPS + 2, *plane),
         *[vmem(*block) for _ in range(5)],
         vmem(NV, *block), vmem(NV, *block),
         vmem(NV, STEPS * STEPS, LANES), vmem(NV, *block),
         vmem(2, *plane), vmem(2, *plane),
+        vmem(NV, *plane), vmem(NV, *plane),
+        vmem(NV, *plane), vmem(NV, *plane), vmem(2, NV, *plane), vmem(NV, *plane),
         vmem(18, *plane), vmem(NV, *plane), vmem(NV, *plane),
         vmem(18, CIRC, LANES), vmem(NV, CIRC, LANES), vmem(NV, CIRC, LANES),
         vmem(NV, CIRC, LANES), vmem(NV, CIRC, LANES), vmem(NV, *plane), vmem(NV, *plane),
@@ -605,12 +698,13 @@
         vmem(mats, *plane), vmem(mats, *plane),
         vmem(12, mats, 8, LANES), vmem(mats, CIRC, LANES),
         vmem(5, CIRC, LANES), vmem(5, CIRC, LANES),
-        vmem(mats, 8, LANES), vmem(mats, 8, LANES), vmem(2, mats, 8, LANES),
-        vmem(*block), vmem(NORM, mats + 2, *plane), vmem(2, NORM, NV, *plane),
+        vmem(mats, 8, LANES), vmem(mats, 8, LANES),
+        vmem(2, mats, 8, LANES), vmem(NORM, *plane), vmem(NORM, 1 + STEPS, *plane),
+        vmem(NORM, mats, *plane), vmem(2, NORM, NV, *plane),
         dma((4,)), dma((1,)), dma((1,)),
         dma((5,)), dma((5,)),
         *[dma((1,)) for _ in range(10)],
-        *[dma((NORM,)) for _ in range(6)],
+        *[dma((NORM,)) for _ in range(8)],
     ]
     anywhere = pl.BlockSpec(memory_space=pltpu.HBM)
     flat = pl.pallas_call(

time: 36.2 us -> 34.8 us (0.961)
  Pallas kernels: 35.3 us -> 33.9 us
    pallas_call x1, Pallas kernels: 35.3 us -> 33.9 us  [per_device(): pl.pallas_call(kernel, out_shape=pltpu.VMEM((NV, STEPS * STEPS, LANES), f...]
where the time goes in v3:
time: 34.8 us; the launch traced here: 34.7 us
  Pallas kernels  33.9 us (97%)
  local copies, waits for them, and re-layouts  0.84 us (2%)
    pallas_call x1, Pallas kernels, per_device(): pl.pallas_call(kernel, out_shape=pltpu.VMEM((NV, STEPS * STEPS, LANES), f...  33.9 us
    unnamed x1, local copies, waits for them, and re-layouts  0.84 us

profile of v3, /device:TPU:1, one launch (start us, length us, event | category | flops | bytes accessed | tf_op | source)
XLA Modules:
  0.0 34.7 jit_solution(2988758127121200543)
XLA Ops:
  0.0 33.9 %shard_map.109 = f32[5,256,128]{2,1,0:T(8,128)S(1)} custom-call(f32[5,16,16,128]{3,2,1,0:T(8,128)} %state.1, f32[16,16,128]{2,1,0:T(8,128)} %visc_in.1, f32[16,16,128]{2,1,0:T(8,128)} %cl_in.1, f32[16,16,128]{2,1,0:T(8,128)} %cu_in.1, f32[16,16,128]{2,1,0:T(8,128)} %nl_in.1, f32[16,16,128]{2,1,0:T(8,128)} %nu_in.1, f32[5,5]{1,0:T(8,128)} %vm_hbm.1, ...), custom_call_target="tpu_custom_call" | custom-call | tf_op jit(solution)/shard_map/pallas_call | solution.py:710
  33.9 0.8 %copy.13 = f32[5,16,16,128]{3,2,1,0:T(8,128)} copy(f32[5,16,16,128]{3,2,1,0:T(8,128)S(1)} %bitcast.1) | data formatting | bytes 1310720

commit v4 on v3

--- a/solution.py
+++ b/solution.py
@@ -12,7 +12,7 @@
 LANES = 128
 OWNERS = 16
 STEP_UNROLL = 16
-SEND_UNROLL = 2
+SEND_UNROLL = 4
 
 
 def place(seg):
@@ -592,6 +592,24 @@
     for d in range(1, NORM):
         pl.when(lax.rem(n + d, NORM) < n)(over_norm(d, bu, bu_send, bu_recv).start)
 
+    to_next.wait_send()
+    to_prev.wait_send()
+    to_side.wait_send()
+    pl.when(has_up)(to_up.wait_send)
+    pl.when(has_down)(to_down.wait_send)
+
+    for way in (w_way, l_way, u_way):
+        whole(*way)[0]()
+
+    @pl.when(owner)
+    def _():
+        for way in (x_way, y_way):
+            whole(*way)[0]()
+
+    for d in range(1, NORM):
+        pl.when(scale_used(n))(over_norm(d, rs, rs_send, rs_recv).wait_send)
+        pl.when(lax.rem(n + d, NORM) < n)(over_norm(d, wn, wn_send, wn_recv).wait_send)
+
     for d in range(1, NORM):
         k = lax.rem(n + d, NORM)
         pl.when(k < n)(from_norm(d, bl, bl_send, bl_recv).wait_recv)
@@ -648,23 +666,7 @@
 
     steps(last_up, start, reverse=True)
 
-    to_next.wait_send()
-    to_prev.wait_send()
-    to_side.wait_send()
-    pl.when(has_up)(to_up.wait_send)
-    pl.when(has_down)(to_down.wait_send)
-
-    for way in (w_way, l_way, u_way):
-        whole(*way)[0]()
-
-    @pl.when(owner)
-    def _():
-        for way in (x_way, y_way):
-            whole(*way)[0]()
-
-    for d in range(1, NORM):
-        pl.when(scale_used(n))(over_norm(d, rs, rs_send, rs_recv).wait_send)
-        pl.when(lax.rem(n + d, NORM) < n)(over_norm(d, wn, wn_send, wn_recv).wait_send)
+    for d in range(1, NORM):
         pl.when(lax.rem(n + d, NORM) > n)(over_norm(d, bl, bl_send, bl_recv).wait_send)
         pl.when(lax.rem(n + d, NORM) < n)(over_norm(d, bu, bu_send, bu_recv).wait_send)
 

time: 34.8 us -> 34.7 us (level)
  no operation moved by 1% of the time
where the time goes in v4:
time: 34.7 us; the launch traced here: 34.6 us
  Pallas kernels  33.8 us (97%)
  local copies, waits for them, and re-layouts  0.84 us (2%)
    pallas_call x1, Pallas kernels, per_device(): pl.pallas_call(kernel, out_shape=pltpu.VMEM((NV, STEPS * STEPS, LANES), f...  33.8 us
    unnamed x1, local copies, waits for them, and re-layouts  0.84 us

profile of v4, /device:TPU:1, one launch (start us, length us, event | category | flops | bytes accessed | tf_op | source)
XLA Modules:
  0.0 34.6 jit_solution(17742173633168751277)
XLA Ops:
  0.0 33.8 %shard_map.109 = f32[5,256,128]{2,1,0:T(8,128)S(1)} custom-call(f32[5,16,16,128]{3,2,1,0:T(8,128)} %state.1, f32[16,16,128]{2,1,0:T(8,128)} %visc_in.1, f32[16,16,128]{2,1,0:T(8,128)} %cl_in.1, f32[16,16,128]{2,1,0:T(8,128)} %cu_in.1, f32[16,16,128]{2,1,0:T(8,128)} %nl_in.1, f32[16,16,128]{2,1,0:T(8,128)} %nu_in.1, f32[5,5]{1,0:T(8,128)} %vm_hbm.1, ...), custom_call_target="tpu_custom_call" | custom-call | tf_op jit(solution)/shard_map/pallas_call | solution.py:712
  33.8 0.8 %copy.13 = f32[5,16,16,128]{3,2,1,0:T(8,128)} copy(f32[5,16,16,128]{3,2,1,0:T(8,128)S(1)} %bitcast.1) | data formatting | bytes 1310720
